TPU v7x, 128 devices: a whole 4x4x4 slice. The times are simulated.
128 devices in a mesh: dp: 16 (over y, z), tp: 8 (over x, core).
Axes of the slice: x: 4, y: 4, z: 4, core: 2. Of those that a mesh axis runs over, the one named last changes fastest.
Arguments:
- cache_pool: bfloat16 [3072, 576, 128], P(('dp', 'tp')), may hold values from -4 to 4
- send_plan: int32 [128, 16, 2], P(('dp', 'tp')), may hold values from -1 to 23, as said below
- tables: int32 [512, 8], P(('dp', 'tp')), may hold values from 0 to 55, as said below
- lengths: int32 [512], P(('dp', 'tp')), may hold values from 385 to 1024
- new_latent: bfloat16 [2, 512, 576], P(None, ('dp', 'tp')), may hold values from -6 to 6
- queries: bfloat16 [2, 512, 64, 576], P(None, ('dp', 'tp')), may hold values from -20 to 20
- value_up: bfloat16 [64, 512, 128], P('dp'), may hold values from -0.25 to 0.25
- out_proj: bfloat16 [8192, 7168], P('dp'), may hold values from -0.0625 to 0.0625
- residual: bfloat16 [2, 512, 7168], P(None, ('dp', 'tp')), may hold values from -3 to 3
- norm_gain: float32 [7168], replicated, may hold values from 0.1 to 1.9
- routes: int32 [2, 512, 8], P(None, ('dp', 'tp')), may hold values from 0 to 31, all different within a row; in each aligned block of 4 rows (0 to 3, 4 to 7, ..., all dimensions but the last counted through in order) at most 2 rows name the same one
- route_weight: float32 [2, 512, 8], P(None, ('dp', 'tp')), may hold values from 0.05 to 0.6
- gate_proj: bfloat16 [32, 7168, 1024], P('dp', None, 'tp'), may hold values from -0.0625 to 0.0625
- up_proj: bfloat16 [32, 7168, 1024], P('dp', None, 'tp'), may hold values from -0.0625 to 0.0625
- down_proj: bfloat16 [32, 1024, 7168], P('dp', 'tp'), may hold values from -0.1875 to 0.1875
Outputs:
- layer_out: bfloat16 [2, 512, 7168], P(None, ('dp', 'tp'))
Inputs may be any that keep to these rules, and one draw needn't show every extreme that they name: `send_plan`: -1 marks an empty slot. A device never lists one of its blocks twice. The blocks that a device sends to index g2 of dp fill its first slots for g2; it sends nothing to its own index of dp; it sends as many blocks in all as it receives; some device fills all 2 slots for a peer. `tables`: the first ceil(lengths[s] / 128) entries of a sequence's row name entries of its device's store after migration; over the device's sequences they name each of its own blocks that it does not send, and each received block that is not empty, exactly once; later entries are 0.
All inputs are finite; a program needn't handle non-finite values.
Results may differ from a plain program's by a relative error of at most 0.024.
Values may be sent and summed in bfloat16 or wider, within the bound.
A program may use at most 192 MiB of HBM per device.

v0:
```python
import jax
import jax.numpy as jnp
from jax import lax
from jax.sharding import PartitionSpec as P

LAT = 512


score_scale = 1.0 / 13.856406460551018
norm_eps = 1e-06


def attend(query_rows, cached_keys, cached_values, usable_mask, fresh_keys):
    cache_scores = (
        jnp.einsum("shc,sbci->shbi", query_rows, cached_keys, preferred_element_type=jnp.float32)
        * score_scale
    )
    cache_scores = jnp.where(usable_mask[:, None], cache_scores, -jnp.inf)
    fresh_scores = (
        jnp.einsum("shc,ksc->shk", query_rows, fresh_keys, preferred_element_type=jnp.float32)
        * score_scale
    )
    largest = jnp.maximum(jnp.max(cache_scores, axis=(2, 3)), jnp.max(fresh_scores, axis=2))
    cache_weights = jnp.exp(cache_scores - largest[:, :, None, None])
    fresh_weights = jnp.exp(fresh_scores - largest[:, :, None])
    denominator = jnp.sum(cache_weights, axis=(2, 3)) + jnp.sum(fresh_weights, axis=2)
    cache_probs = (cache_weights / denominator[:, :, None, None]).astype(jnp.bfloat16)
    fresh_probs = (fresh_weights / denominator[:, :, None]).astype(jnp.bfloat16)
    latent_sum = jnp.einsum(
        "shbi,sbci->shc", cache_probs, cached_values, preferred_element_type=jnp.float32
    )
    latent_sum = latent_sum + jnp.einsum(
        "shk,ksc->shc", fresh_probs, fresh_keys[:, :, :LAT], preferred_element_type=jnp.float32
    )
    return latent_sum.astype(jnp.bfloat16)


def run_experts(expert_rows, gate_proj, up_proj, down_proj):
    gate_act = jnp.einsum(
        "erd,edh->erh", expert_rows, gate_proj, preferred_element_type=jnp.float32
    )
    up_act = jnp.einsum("erd,edh->erh", expert_rows, up_proj, preferred_element_type=jnp.float32)
    hidden = (jax.nn.silu(gate_act) * up_act).astype(jnp.bfloat16)
    return jnp.einsum("erh,ehd->erd", hidden, down_proj, preferred_element_type=jnp.float32).astype(
        jnp.bfloat16
    )


def per_device(
    cache_pool,
    send_plan,
    tables,
    lengths,
    new_latent,
    queries,
    value_up,
    out_proj,
    residual,
    norm_gain,
    routes,
    route_weight,
    gate_proj,
    up_proj,
    down_proj,
):
    group_count = lax.axis_size("dp")
    lane_count = lax.axis_size("tp")
    pool_blocks, lat_width, block_tokens = cache_pool.shape
    slot_count = send_plan.shape[2]
    flat_pool = cache_pool.reshape(pool_blocks, lat_width * block_tokens)
    picker = (
        send_plan.reshape(-1)[:, None] == jnp.arange(pool_blocks, dtype=jnp.int32)[None, :]
    ).astype(jnp.bfloat16)
    outgoing = jnp.dot(picker, flat_pool, preferred_element_type=jnp.float32).astype(jnp.bfloat16)
    outgoing = outgoing.reshape(group_count, slot_count, lat_width, block_tokens)
    arrived = lax.all_to_all(outgoing, "dp", split_axis=0, concat_axis=0, tiled=True)
    combined = jnp.concatenate(
        [cache_pool, arrived.reshape(group_count * slot_count, lat_width, block_tokens)], axis=0
    )
    cached_keys = jnp.take(combined, tables, axis=0)
    cached_values = cached_keys[:, :, :LAT, :]
    table_width = tables.shape[1]
    token_position = (
        jnp.arange(table_width, dtype=jnp.int32)[:, None] * block_tokens
        + jnp.arange(block_tokens, dtype=jnp.int32)[None, :]
    )
    usable_mask = token_position[None] < lengths[:, None, None]
    seq_dev = routes.shape[1]
    top_count = routes.shape[2]
    model_width = residual.shape[2]
    expert_here = gate_proj.shape[0]
    expert_total = group_count * expert_here
    capacity = min(seq_dev, max(2, -(-(2 * seq_dev * top_count) // expert_total)))
    expert_range = jnp.arange(expert_total, dtype=jnp.int32)
    slot_range = jnp.arange(capacity, dtype=jnp.int32)
    results = []
    for step_no in range(residual.shape[0]):
        latent_out = attend(
            queries[step_no], cached_keys, cached_values, usable_mask, new_latent[: step_no + 1]
        )
        head_rows = lax.all_to_all(latent_out, "dp", split_axis=1, concat_axis=0, tiled=True)
        per_head = jnp.einsum(
            "shc,hcv->shv", head_rows, value_up, preferred_element_type=jnp.float32
        ).astype(jnp.bfloat16)
        head_flat = per_head.reshape(per_head.shape[0], per_head.shape[1] * per_head.shape[2])
        attention = lax.psum_scatter(
            jnp.dot(head_flat, out_proj, preferred_element_type=jnp.float32).astype(jnp.bfloat16),
            "dp",
            scatter_dimension=0,
            tiled=True,
        ).astype(jnp.float32)
        stream = (residual[step_no].astype(jnp.float32) + attention).astype(jnp.bfloat16)
        stream_wide = stream.astype(jnp.float32)
        mean_square = jnp.mean(stream_wide * stream_wide, axis=1, keepdims=True)
        normed = (stream_wide * lax.rsqrt(mean_square + norm_eps) * norm_gain).astype(jnp.bfloat16)
        expert_ids = routes[step_no]
        matches = expert_ids[:, :, None] == expert_range[None, None, :]
        chosen = jnp.sum(matches.astype(jnp.int32), axis=1)
        earlier = jnp.cumsum(chosen, axis=0) - chosen
        placement = (
            (earlier[:, :, None] == slot_range[None, None, :]) & (chosen[:, :, None] > 0)
        ).astype(jnp.bfloat16)
        outbound = jnp.einsum(
            "sec,sd->ecd", placement, normed, preferred_element_type=jnp.float32
        ).astype(jnp.bfloat16)
        spread = jnp.broadcast_to(
            outbound.reshape(group_count, 1, expert_here, capacity, model_width),
            (group_count, lane_count, expert_here, capacity, model_width),
        )
        spread = spread.reshape(group_count * lane_count, expert_here, capacity, model_width)
        inbound = lax.all_to_all(spread, ("dp", "tp"), split_axis=0, concat_axis=0, tiled=True)
        expert_rows = jnp.transpose(inbound, (1, 0, 2, 3)).reshape(
            expert_here, group_count * lane_count * capacity, model_width
        )
        produced = run_experts(expert_rows, gate_proj, up_proj, down_proj)
        lane_major = jnp.transpose(
            produced.reshape(expert_here, group_count, lane_count, capacity, model_width),
            (2, 1, 0, 3, 4),
        )
        sendback = jnp.transpose(lane_major, (1, 0, 2, 3, 4)).reshape(
            group_count * lane_count, expert_here, capacity, model_width
        )
        returned = lax.all_to_all(sendback, ("dp", "tp"), split_axis=0, concat_axis=0, tiled=True)
        partials = returned.reshape(group_count, lane_count, expert_here, capacity, model_width)
        summed = jnp.sum(partials.astype(jnp.float32), axis=1).reshape(
            expert_total * capacity, model_width
        )
        slot_of = jnp.sum(jnp.where(matches, earlier[:, None, :], 0), axis=2)
        flat_index = (expert_ids * capacity + slot_of).reshape(-1)
        picked = jnp.take(summed, flat_index, axis=0).reshape(seq_dev, top_count, model_width)
        mixture = jnp.sum(picked * route_weight[step_no][:, :, None], axis=1)
        results.append((stream_wide + mixture).astype(jnp.bfloat16))
    return jnp.stack(results)


def solution(mesh):
    placed = (
        P(("dp", "tp"), None, None),
        P(("dp", "tp"), None, None),
        P(("dp", "tp"), None),
        P(("dp", "tp")),
        P(None, ("dp", "tp"), None),
        P(None, ("dp", "tp"), None, None),
        P("dp", None, None),
        P("dp", None),
        P(None, ("dp", "tp"), None),
        P(),
        P(None, ("dp", "tp"), None),
        P(None, ("dp", "tp"), None),
        P("dp", None, "tp"),
        P("dp", None, "tp"),
        P("dp", "tp", None),
    )
    return jax.shard_map(
        per_device,
        mesh=mesh,
        in_specs=placed,
        out_specs=P(None, ("dp", "tp"), None),
        check_vma=False,
    )
```

profile of v0, /device:TPU:0, one launch (start us, length us, event | category | flops | bytes accessed | tf_op | source)
XLA Modules:
  0.0 678.7 jit_solution(2091351977127526284)
XLA Ops:
  15.4 8.3 %all-to-all-start = ((bf16[16,2,576,128]{3,2,1,0:T(8,128)(2,1)}), bf16[16,2,576,128]{3,2,1,0:T(8,128)(2,1)}, u32[]{:S(2)}, u32[]{:S(2)}) async-start(bf16[16,2,576,128]{3,2,1,0:T(8,128)(2,1)} %bitcast.158), calls=%async_computation | async-start | bytes 9437184 | tf_op jit(solution)/shard_map/all_to_all | solution.py:76
  24.5 72.5 %all-to-all-done = bf16[16,2,576,128]{3,2,1,0:T(8,128)(2,1)} async-done(((bf16[16,2,576,128]{3,2,1,0:T(8,128)(2,1)}), bf16[16,2,576,128]{3,2,1,0:T(8,128)(2,1)}, u32[]{:S(2)}, u32[]{:S(2)}) %all-to-all-start) | async-done | bytes 4718624 | tf_op jit(solution)/shard_map/all_to_all | solution.py:76
  119.0 9.6 %all-to-all-start.4 = ((bf16[4,64,512]{2,0,1:T(4,128)(2,1)}), bf16[4,64,512]{2,0,1:T(4,128)(2,1)S(1)}, u32[]{:S(2)}, u32[]{:S(2)}) async-start(bf16[4,64,512]{2,0,1:T(4,128)(2,1)} %copy.62), calls=%async_computation.4 | async-start | bytes 524288 | tf_op jit(solution)/shard_map/all_to_all | solution.py:101
  141.1 8.1 %all-to-all-done.1 = bf16[4,64,512]{2,0,1:T(4,128)(2,1)S(1)} async-done(((bf16[4,64,512]{2,0,1:T(4,128)(2,1)}), bf16[4,64,512]{2,0,1:T(4,128)(2,1)S(1)}, u32[]{:S(2)}, u32[]{:S(2)}) %all-to-all-start.1) | async-done | bytes 262176 | tf_op jit(solution)/shard_map/all_to_all | solution.py:101
  159.3 86.5 %all-reduce.5.cloned.1.call-done = (bf16[64,7168]{1,0:T(8,128)(2,1)}, bf16[64,7168]{1,0:T(8,128)(2,1)}) async-done(((bf16[64,7168]{1,0:T(8,128)(2,1)}, bf16[64,7168]{1,0:T(8,128)(2,1)}), (bf16[64,7168]{1,0:T(8,128)(2,1)}, bf16[64,7168]{1,0:T(8,128)(2,1)})) %all-reduce.5.cloned.1.call-update) | async-done | bytes 1835024
  254.0 8.3 %all-to-all-start.2 = ((bf16[128,2,2,7168]{3,2,1,0:T(2,128)(2,1)}), bf16[128,2,2,7168]{3,2,1,0:T(2,128)(2,1)}, u32[]{:S(2)}, u32[]{:S(2)}) async-start(bf16[128,2,2,7168]{3,2,1,0:T(2,128)(2,1)} %bitcast.155), calls=%async_computation.2 | async-start | bytes 14680064 | tf_op jit(solution)/shard_map/all_to_all | solution.py:131
  263.9 86.9 %all-to-all-done.2 = bf16[128,2,2,7168]{3,2,1,0:T(2,128)(2,1)} async-done(((bf16[128,2,2,7168]{3,2,1,0:T(2,128)(2,1)}), bf16[128,2,2,7168]{3,2,1,0:T(2,128)(2,1)}, u32[]{:S(2)}, u32[]{:S(2)}) %all-to-all-start.2) | async-done | bytes 7340064 | tf_op jit(solution)/shard_map/all_to_all | solution.py:131
  356.3 11.2 %all-to-all-start.5 = ((bf16[128,2,2,7168]{3,2,1,0:T(2,128)(2,1)}), bf16[128,2,2,7168]{3,2,1,0:T(2,128)(2,1)}, u32[]{:S(2)}, u32[]{:S(2)}) async-start(bf16[128,2,2,7168]{3,2,1,0:T(2,128)(2,1)} %bitcast.156), calls=%async_computation.5 | async-start | bytes 14680064 | tf_op jit(solution)/shard_map/all_to_all | solution.py:131
  374.7 15.5 %reshape.218 = bf16[2,256,7168]{2,1,0:T(8,128)(2,1)} reshape(bf16[2,128,2,7168]{3,2,1,0:T(2,128)(2,1)} %copy.56) | data formatting | bytes 14680064 | tf_op jit(solution)/shard_map/reshape | solution.py:132
  396.4 12.2 %convolution_convert_fusion.2 = bf16[2,256,7168]{2,1,0:T(8,128)(2,1)} fusion(bf16[2,128,7168]{2,1,0:T(8,128)(2,1)} %param.31, bf16[2,256,7168]{2,1,0:T(8,128)(2,1)} %reshape.218, bf16[2,7168,128]{2,1,0:T(8,128)(2,1)} %param.30, f32[2,256,128]{2,1,0:T(8,128)S(1)} %fusion.107), kind=kOutput, calls=%fused_computation.7 | convolution fusion | flops 1883111424 | bytes 22282240 | tf_op jit(solution)/shard_map/erh,ehd->erd/dot_general | solution.py:44
  408.6 14.9 %reshape.219 = bf16[2,16,8,2,7168]{4,3,2,1,0:T(2,128)(2,1)} reshape(bf16[2,256,7168]{2,1,0:T(8,128)(2,1)} %convolution_convert_fusion.2) | data formatting | bytes 14680064 | tf_op jit(solution)/shard_map/reshape | solution.py:137
  423.5 8.2 %copy.57 = bf16[16,8,2,2,7168]{4,3,2,1,0:T(2,128)(2,1)} copy(bf16[16,8,2,2,7168]{4,3,1,0,2:T(2,128)(2,1)} %bitcast.153) | data formatting | bytes 14680064 | tf_op jit(solution)/shard_map/transpose;transpose | solution.py:140
  431.7 23.8 %all-to-all-done.5 = bf16[128,2,2,7168]{3,2,1,0:T(2,128)(2,1)} async-done(((bf16[128,2,2,7168]{3,2,1,0:T(2,128)(2,1)}), bf16[128,2,2,7168]{3,2,1,0:T(2,128)(2,1)}, u32[]{:S(2)}, u32[]{:S(2)}) %all-to-all-start.5) | async-done | bytes 7340064 | tf_op jit(solution)/shard_map/all_to_all | solution.py:131
  455.5 11.0 %all-to-all-start.3 = ((bf16[128,2,2,7168]{3,2,1,0:T(2,128)(2,1)}), bf16[128,2,2,7168]{3,2,1,0:T(2,128)(2,1)}, u32[]{:S(2)}, u32[]{:S(2)}) async-start(bf16[128,2,2,7168]{3,2,1,0:T(2,128)(2,1)} %bitcast.152), calls=%async_computation.3 | async-start | bytes 14680064 | tf_op jit(solution)/shard_map/all_to_all | solution.py:143
  466.5 7.3 %copy.66 = bf16[2,128,2,7168]{3,2,1,0:T(2,128)(2,1)} copy(bf16[2,128,2,7168]{3,2,0,1:T(2,128)(2,1)} %bitcast.42) | data formatting | bytes 14680064 | tf_op jit(solution)/shard_map/transpose | solution.py:132
  473.8 15.4 %reshape.225 = bf16[2,256,7168]{2,1,0:T(8,128)(2,1)} reshape(bf16[2,128,2,7168]{3,2,1,0:T(2,128)(2,1)} %copy.66) | data formatting | bytes 14680064 | tf_op jit(solution)/shard_map/reshape | solution.py:132
  495.4 12.2 %convolution_convert_fusion.1 = bf16[2,256,7168]{2,1,0:T(8,128)(2,1)} fusion(bf16[2,128,7168]{2,1,0:T(8,128)(2,1)} %param.31, bf16[2,256,7168]{2,1,0:T(8,128)(2,1)} %reshape.225, bf16[2,7168,128]{2,1,0:T(8,128)(2,1)} %param.30, f32[2,256,128]{2,1,0:T(8,128)S(1)} %fusion.108), kind=kOutput, calls=%fused_computation.6 | convolution fusion | flops 1883111424 | bytes 22282240 | tf_op jit(solution)/shard_map/erh,ehd->erd/dot_general | solution.py:44
  507.6 14.9 %reshape.226 = bf16[2,16,8,2,7168]{4,3,2,1,0:T(2,128)(2,1)} reshape(bf16[2,256,7168]{2,1,0:T(8,128)(2,1)} %convolution_convert_fusion.1) | data formatting | bytes 14680064 | tf_op jit(solution)/shard_map/reshape | solution.py:137
  522.5 8.2 %copy.67 = bf16[16,8,2,2,7168]{4,3,2,1,0:T(2,128)(2,1)} copy(bf16[16,8,2,2,7168]{4,3,1,0,2:T(2,128)(2,1)} %bitcast.154) | data formatting | bytes 14680064 | tf_op jit(solution)/shard_map/transpose;transpose | solution.py:140
  530.7 23.8 %all-to-all-done.3 = bf16[128,2,2,7168]{3,2,1,0:T(2,128)(2,1)} async-done(((bf16[128,2,2,7168]{3,2,1,0:T(2,128)(2,1)}), bf16[128,2,2,7168]{3,2,1,0:T(2,128)(2,1)}, u32[]{:S(2)}, u32[]{:S(2)}) %all-to-all-start.3) | async-done | bytes 7340064 | tf_op jit(solution)/shard_map/all_to_all | solution.py:143
  554.5 10.7 %all-to-all-start.6 = ((bf16[128,2,2,7168]{3,2,1,0:T(2,128)(2,1)}), bf16[128,2,2,7168]{3,2,1,0:T(2,128)(2,1)}, u32[]{:S(2)}, u32[]{:S(2)}) async-start(bf16[128,2,2,7168]{3,2,1,0:T(2,128)(2,1)} %bitcast.151), calls=%async_computation.6 | async-start | bytes 14680064 | tf_op jit(solution)/shard_map/all_to_all | solution.py:143
  566.1 9.8 %convert_reduce_fusion.1 = f32[16,2,2,7168]{3,2,1,0:T(2,128)} fusion(bf16[128,2,2,7168]{3,2,1,0:T(2,128)(2,1)} %all-to-all-done.3), kind=kLoop, calls=%fused_computation.5 | loop fusion | flops 6881280 | bytes 9175040 | tf_op jit(solution)/shard_map/reduce_sum | solution.py:145
  578.5 74.8 %all-to-all-done.6 = bf16[128,2,2,7168]{3,2,1,0:T(2,128)(2,1)} async-done(((bf16[128,2,2,7168]{3,2,1,0:T(2,128)(2,1)}), bf16[128,2,2,7168]{3,2,1,0:T(2,128)(2,1)}, u32[]{:S(2)}, u32[]{:S(2)}) %all-to-all-start.6) | async-done | bytes 7340064 | tf_op jit(solution)/shard_map/all_to_all | solution.py:143
  653.4 9.8 %convert_reduce_fusion = f32[16,2,2,7168]{3,2,1,0:T(2,128)} fusion(bf16[128,2,2,7168]{3,2,1,0:T(2,128)(2,1)} %all-to-all-done.6), kind=kLoop, calls=%fused_computation.4 | loop fusion | flops 6881280 | bytes 9175040 | tf_op jit(solution)/shard_map/reduce_sum | solution.py:145
  (115 shorter events, 100.2 us)
Async XLA Ops:
  6.5 142.8 %copy-start = (bf16[4,512,128]{2,1,0:T(8,128)(2,1)S(1)}, bf16[4,512,128]{2,1,0:T(8,128)(2,1)}, u32[]{:S(2)}) copy-start(bf16[4,512,128]{2,1,0:T(8,128)(2,1)} %param.23) | copy-start | bytes 1572868
  15.3 8.3 %copy-start.7 = (s32[4,8]{1,0:T(4,128)S(1)}, s32[4,8]{1,0:T(4,128)}, u32[]{:S(2)}) copy-start(s32[4,8]{1,0:T(4,128)} %param.19) | copy-start | bytes 388
  15.3 8.4 %copy-start.6 = (bf16[2,4,576]{2,1,0:T(4,128)(2,1)S(1)}, bf16[2,4,576]{2,1,0:T(4,128)(2,1)}, u32[]{:S(2)}) copy-start(bf16[2,4,576]{2,1,0:T(4,128)(2,1)} %param.21) | copy-start | bytes 27652
  15.3 8.6 %copy-start.10 = (s32[4]{0:T(128)S(1)}, s32[4]{0:T(128)}, u32[]{:S(2)}) copy-start(s32[4]{0:T(128)} %param.20) | copy-start | bytes 52
  15.4 8.7 %copy-start.3 = (bf16[2,4,64,576]{3,2,1,0:T(8,128)(2,1)S(1)}, bf16[2,4,64,576]{3,2,1,0:T(8,128)(2,1)}, u32[]{:S(2)}) copy-start(bf16[2,4,64,576]{3,2,1,0:T(8,128)(2,1)} %param.22) | copy-start | bytes 1769476
  15.4 81.6 %all-to-all-start = ((bf16[16,2,576,128]{3,2,1,0:T(8,128)(2,1)}), bf16[16,2,576,128]{3,2,1,0:T(8,128)(2,1)}, u32[]{:S(2)}, u32[]{:S(2)}) async-start(bf16[16,2,576,128]{3,2,1,0:T(8,128)(2,1)} %bitcast.158), calls=%async_computation | async-start | bytes 9437184 | tf_op jit(solution)/shard_map/all_to_all | solution.py:76
  113.8 2.6 copy-start.2
  119.0 18.0 %all-to-all-start.4 = ((bf16[4,64,512]{2,0,1:T(4,128)(2,1)}), bf16[4,64,512]{2,0,1:T(4,128)(2,1)S(1)}, u32[]{:S(2)}, u32[]{:S(2)}) async-start(bf16[4,64,512]{2,0,1:T(4,128)(2,1)} %copy.62), calls=%async_computation.4 | async-start | bytes 524288 | tf_op jit(solution)/shard_map/all_to_all | solution.py:101
  137.0 12.1 %all-to-all-start.1 = ((bf16[4,64,512]{2,0,1:T(4,128)(2,1)}), bf16[4,64,512]{2,0,1:T(4,128)(2,1)S(1)}, u32[]{:S(2)}, u32[]{:S(2)}) async-start(bf16[4,64,512]{2,0,1:T(4,128)(2,1)} %copy.52), calls=%async_computation.1 | async-start | bytes 524288 | tf_op jit(solution)/shard_map/all_to_all | solution.py:101
  140.7 105.1 %all-reduce.5.cloned.1.call-start = ((), (), s32[]{:S(2)}) async-start(), calls=%async_computation.7 | async-start | bytes 3670016
  149.3 6.2 slice-start
  149.8 5.7 slice-start.1
  155.5 2.4 copy-start.8
  155.5 2.6 copy-start.11
  155.5 90.3 %copy-start.4 = (bf16[2,4,7168]{2,1,0:T(4,128)(2,1)S(1)}, bf16[2,4,7168]{2,1,0:T(4,128)(2,1)}, u32[]{:S(2)}) copy-start(bf16[2,4,7168]{2,1,0:T(4,128)(2,1)} %param.25) | copy-start | bytes 344068
  155.5 91.5 %copy-start.5 = (f32[7168]{0:T(1024)S(1)}, f32[7168]{0:T(1024)}, u32[]{:S(2)}) copy-start(f32[7168]{0:T(1024)} %param.26) | copy-start | bytes 86020
  254.0 96.7 %all-to-all-start.2 = ((bf16[128,2,2,7168]{3,2,1,0:T(2,128)(2,1)}), bf16[128,2,2,7168]{3,2,1,0:T(2,128)(2,1)}, u32[]{:S(2)}, u32[]{:S(2)}) async-start(bf16[128,2,2,7168]{3,2,1,0:T(2,128)(2,1)} %bitcast.155), calls=%async_computation.2 | async-start | bytes 14680064 | tf_op jit(solution)/shard_map/all_to_all | solution.py:131
  356.3 99.2 %all-to-all-start.5 = ((bf16[128,2,2,7168]{3,2,1,0:T(2,128)(2,1)}), bf16[128,2,2,7168]{3,2,1,0:T(2,128)(2,1)}, u32[]{:S(2)}, u32[]{:S(2)}) async-start(bf16[128,2,2,7168]{3,2,1,0:T(2,128)(2,1)} %bitcast.156), calls=%async_computation.5 | async-start | bytes 14680064 | tf_op jit(solution)/shard_map/all_to_all | solution.py:131
  455.5 99.1 %all-to-all-start.3 = ((bf16[128,2,2,7168]{3,2,1,0:T(2,128)(2,1)}), bf16[128,2,2,7168]{3,2,1,0:T(2,128)(2,1)}, u32[]{:S(2)}, u32[]{:S(2)}) async-start(bf16[128,2,2,7168]{3,2,1,0:T(2,128)(2,1)} %bitcast.152), calls=%async_computation.3 | async-start | bytes 14680064 | tf_op jit(solution)/shard_map/all_to_all | solution.py:143
  554.5 11.6 %copy-start.9 = (f32[2,4,8]{2,1,0:T(4,128)S(1)}, f32[2,4,8]{2,1,0:T(4,128)}, u32[]{:S(2)}) copy-start(f32[2,4,8]{2,1,0:T(4,128)} %param.28) | copy-start | bytes 772
  554.5 98.8 %all-to-all-start.6 = ((bf16[128,2,2,7168]{3,2,1,0:T(2,128)(2,1)}), bf16[128,2,2,7168]{3,2,1,0:T(2,128)(2,1)}, u32[]{:S(2)}, u32[]{:S(2)}) async-start(bf16[128,2,2,7168]{3,2,1,0:T(2,128)(2,1)} %bitcast.151), calls=%async_computation.6 | async-start | bytes 14680064 | tf_op jit(solution)/shard_map/all_to_all | solution.py:143
  666.5 5.2 copy-start.1
Sparse Core Ops, SparseCore 0:
  158.0 87.7 all-reduce.4
where the time goes:
time: 692 us; the launch traced here: 679 us
  waiting for transfers between devices  380 us (55%)
  local copies, waits for them, and re-layouts  128 us (18%)
  starting transfers between devices  62.9 us (9%)
  matrix products  58.8 us (8%)
  other arithmetic  34.1 us (5%)
  between operations  14.7 us (2%)
    all_to_all x2, waiting for transfers between devices, per_device(): lax.all_to_all(spread, ('dp', 'tp'), split_axis=0, concat_axis=0, tiled=T...  111 us
    all_to_all x2, waiting for transfers between devices, per_device(): lax.all_to_all(sendback, ('dp', 'tp'), split_axis=0, concat_axis=0, tiled...  98.7 us
    unnamed x2, waiting for transfers between devices  86.5 us
    all_to_all x1, waiting for transfers between devices, per_device(): lax.all_to_all(outgoing, 'dp', split_axis=0, concat_axis=0, tiled=True)  72.5 us
    reshape x2, local copies, waits for them, and re-layouts, per_device(): jnp.transpose(inbound, (1, 0, 2, 3))  30.9 us
    reshape x2, local copies, waits for them, and re-layouts, per_device(): produced.reshape(expert_here, group_count, lane_count, capacity, model_wi...  29.8 us
    dot_general x2, matrix products, run_experts(): jnp.einsum('erh,ehd->erd', hidden, down_proj, preferred_element_type=jnp....  24.4 us
    all_to_all x2, starting transfers between devices, per_device(): lax.all_to_all(sendback, ('dp', 'tp'), split_axis=0, concat_axis=0, tiled...  21.7 us
  transfers between devices with their start and end apart: 8, of which 8 were waited for; matrix products, arithmetic and copies ran while one was open for 22% of the time, Pallas kernels for 0%

commit v1 on v0

v1 whole, which is shorter than its diff:
```python
import functools

import jax
import jax.numpy as jnp
from jax import lax
from jax.experimental import pallas as pl
from jax.experimental.pallas import tpu as pltpu
from jax.sharding import PartitionSpec as P

MESH = pl.DeviceIdType.MESH
F32 = jnp.float32
BF16 = jnp.bfloat16
LAT = 512
SCALE = 1.0 / 13.856406460551018
EPS = 1e-06
MIB = 1 << 20


def dot(a, b):
    return jnp.dot(a, b, preferred_element_type=F32)


def dot_nt(a, b):
    return lax.dot_general(a, b, (((1,), (1,)), ((), ())), preferred_element_type=F32)


def attention_kernel(
    plan, tab, lens, pool, queries, fresh, value_up, proj_hbm, resid, gain,
    stream_out, normed_out,
    outgoing, arrived, keys, lat_send, lat_recv, proj, part_send, part_recv,
    mig_send, mig_recv, lat_s, lat_r, part_s, part_r, local_sem,
):
    groups = 16
    me = lax.axis_index("dp")
    lane = lax.axis_index("tp")
    model = proj_hbm.shape[1]

    proj_copy = pltpu.make_async_copy(proj_hbm, proj, local_sem.at[0])
    proj_copy.start()

    barrier = pltpu.get_barrier_semaphore()
    for shift in range(1, groups):
        pl.semaphore_signal(
            barrier, inc=1, device_id=(lax.rem(me + shift, groups), lane), device_id_type=MESH
        )

    def pick(i, carry):
        outgoing[i] = pool[jnp.maximum(plan[i], 0)]
        return carry

    lax.fori_loop(0, 2 * groups, pick, 0)
    pl.semaphore_wait(barrier, groups - 1)

    def exchange(src, dst, send_sem, recv_sem, shift):
        peer = lax.rem(me + shift, groups)
        return pltpu.make_async_remote_copy(
            src_ref=src(peer),
            dst_ref=dst(me),
            send_sem=send_sem.at[shift - 1],
            recv_sem=recv_sem.at[shift - 1],
            device_id=(peer, lane),
            device_id_type=MESH,
        )

    moves = [
        exchange(
            lambda p: outgoing.at[pl.ds(2 * p, 2)],
            lambda m: arrived.at[pl.ds(2 * m, 2)],
            mig_send, mig_recv, shift,
        )
        for shift in range(1, groups)
    ]
    for move in moves:
        move.start()
    arrived[2 * me] = outgoing[2 * me]
    arrived[2 * me + 1] = outgoing[2 * me + 1]
    for move in moves:
        move.wait()

    row = lax.broadcasted_iota(jnp.int32, (128, 128), 0)
    col = lax.broadcasted_iota(jnp.int32, (128, 128), 1)
    reorder = jnp.where(
        col == ((row >> 2) & 1) * 64 + (row >> 3) * 4 + (row & 3), 1.0, 0.0
    ).astype(BF16)
    second_step = ((lax.broadcasted_iota(jnp.int32, (128, 1), 0) >> 2) & 1) == 1
    position = lax.broadcasted_iota(jnp.int32, (128, 1024), 1)

    def attend(s, carry):
        for j in range(8):
            entry = tab[s * 8 + j]
            own = pool[jnp.minimum(entry, 23)]
            moved = arrived[jnp.maximum(entry - 24, 0)]
            keys[:, j * 128:(j + 1) * 128] = jnp.where(entry < 24, own, moved)
        q = jnp.concatenate([queries[0, s], queries[1, s]], axis=0)
        q = dot(reorder, q)
        q16 = q.astype(BF16)
        scores = dot(q16, keys[...]) * SCALE
        scores = jnp.where(position < lens[s], scores, -jnp.inf)
        new = fresh[s]
        first = jnp.sum(q * new[0:1], axis=1, keepdims=True) * SCALE
        second = jnp.sum(q * new[1:2], axis=1, keepdims=True) * SCALE
        second = jnp.where(second_step, second, -jnp.inf)
        largest = jnp.maximum(jnp.max(scores, axis=1, keepdims=True), jnp.maximum(first, second))
        weights = jnp.exp(scores - largest)
        first = jnp.exp(first - largest)
        second = jnp.exp(second - largest)
        total = jnp.sum(weights, axis=1, keepdims=True) + first + second
        probs = (weights / total).astype(BF16)
        first = (first / total).astype(BF16).astype(F32)
        second = (second / total).astype(BF16).astype(F32)
        latent = dot_nt(probs, keys[0:LAT, :])
        latent = latent + first * new[0:1, 0:LAT] + second * new[1:2, 0:LAT]
        lat_send[:, pl.ds(s, 1)] = latent.reshape(16, 1, 8, LAT).astype(BF16)
        return carry

    lax.fori_loop(0, 4, attend, 0)

    moves = [
        exchange(lambda p: lat_send.at[p], lambda m: lat_recv.at[m], lat_s, lat_r, shift)
        for shift in range(1, groups)
    ]
    for move in moves:
        move.start()
    lat_recv[me] = lat_send[me]
    for move in moves:
        move.wait()

    rows = lat_recv[...].astype(F32).reshape(512, LAT).astype(BF16)
    row = lax.broadcasted_iota(jnp.int32, (128, 512), 0)
    col = lax.broadcasted_iota(jnp.int32, (128, 512), 1)
    base = (row >> 3) * 32 + (row & 3) * 8 + ((row >> 2) & 1) * 4
    heads = []
    for h in range(4):
        up = dot(rows, value_up[h]).astype(BF16)
        take = jnp.where(col == base + h, 1.0, 0.0).astype(BF16)
        heads.append(dot(take, up).astype(BF16))
    heads = jnp.concatenate(heads, axis=1)
    proj_copy.wait()
    chunk = 1024
    for n in range(model // chunk):
        cols = pl.ds(n * chunk, chunk)
        part_send[:, :, cols] = dot(heads, proj[:, cols]).reshape(16, 8, chunk).astype(BF16)

    moves = [
        exchange(lambda p: part_send.at[p], lambda m: part_recv.at[m], part_s, part_r, shift)
        for shift in range(1, groups)
    ]
    for move in moves:
        move.start()
    part_recv[me] = part_send[me]
    for move in moves:
        move.wait()

    square = jnp.zeros((8, 1), F32)
    for n in range(model // chunk):
        cols = pl.ds(n * chunk, chunk)
        total = resid[:, cols].astype(F32) + jnp.sum(part_recv[:, :, cols].astype(F32), axis=0)
        stream = total.astype(BF16)
        stream_out[:, cols] = stream
        wide = stream.astype(F32)
        square = square + jnp.sum(wide * wide, axis=1, keepdims=True)
    scale = lax.rsqrt(square * (1.0 / model) + EPS)
    for n in range(model // chunk):
        cols = pl.ds(n * chunk, chunk)
        wide = stream_out[:, cols].astype(F32)
        normed_out[:, cols] = (wide * scale * gain[:, cols]).astype(BF16)


PARTS = ((0, 2432), (2432, 2432), (4864, 2432))
OUT_PARTS = ((0, 2432), (2432, 2432), (4864, 2304))
ROW = 7296


def halves(start, width):
    tiles = width // 128
    first = (tiles + 1) // 2 * 128
    return (start, first), (start + first, width - first)


def expert_kernel(
    normed, mix, stream, gate, up, down,
    out,
    rows_buf, rows, hid_w, down_w, acc, obuf,
    h0l, h0r, f0l, f0r, h1l, h1r, f1l, f1r, h2l, h2r, f2l, f2r,
    ag_send, ag_recv, rs_send, rs_recv, w_send, w_recv, w_local,
):
    dp = lax.axis_index("dp")
    tp = lax.axis_index("tp")
    at = (dp // 4, dp % 4, tp // 2)
    core = tp % 2

    def neighbour(axis, sign):
        new = list(at)
        new[axis] = (at[axis] + sign + 4) % 4
        return (new[0] * 4 + new[1], new[2] * 2 + core)

    partner = (dp, (tp // 2) * 2 + (1 - core))

    barrier = pltpu.get_barrier_semaphore()
    for axis in range(3):
        for sign in (1, -1):
            pl.semaphore_signal(
                barrier, inc=1, device_id=neighbour(axis, sign), device_id_type=MESH
            )
    pl.semaphore_signal(barrier, inc=1, device_id=partner, device_id_type=MESH)

    rows_buf[at[0], at[1], at[2], :, 0:7168] = normed[...]
    rows_buf[at[0], at[1], at[2], :, 7168:7296] = mix[...]
    local = []
    remote = []

    def spots(e, which):
        if which < 2:
            base = e * 512 + which * 256
            return (
                hid_w.at[:, pl.ds(base, 128)],
                hid_w.at[:, pl.ds(base + 128, 128)],
            )
        return (
            down_w.at[pl.ds(e * 256, 128)],
            down_w.at[pl.ds(e * 256 + 128, 128)],
        )

    for e in range(2):
        for which, ref in enumerate((gate, up, down)):
            mine, theirs = spots(e, which)
            n = e * 3 + which
            local.append(pltpu.make_async_copy(ref.at[e], mine, w_local.at[n]))
            remote.append(
                pltpu.make_async_remote_copy(
                    src_ref=ref.at[e],
                    dst_ref=theirs,
                    send_sem=w_send.at[n],
                    recv_sem=w_recv.at[n],
                    device_id=partner,
                    device_id_type=MESH,
                )
            )
    for copy in local:
        copy.start()
    pl.semaphore_wait(barrier, 7)

    order = [(p, (p + 1) % 3, (p + 2) % 3) for p in range(3)]

    def place(known, axis, value):
        where = [at[0], at[1], at[2]]
        for a in known:
            where[a] = slice(None)
        where[axis] = value
        return tuple(where)

    def push(ref, dst, sends, recvs, slot, axis, sign):
        return pltpu.make_async_remote_copy(
            src_ref=ref,
            dst_ref=dst,
            send_sem=sends.at[slot],
            recv_sem=recvs.at[slot],
            device_id=neighbour(axis, sign),
            device_id_type=MESH,
        )

    for phase in range(3):
        ones = []
        for p in range(3):
            axis = order[p][phase]
            known = order[p][:phase]
            start, width = PARTS[p]
            own = place(known, axis, at[axis]) + (slice(None), pl.ds(start, width))
            slot = (phase * 3 + p) * 4
            pair = [
                push(rows_buf.at[own], rows_buf.at[own], ag_send, ag_recv, slot + k, axis, sign)
                for k, sign in enumerate((1, -1))
            ]
            for copy in pair:
                copy.start()
            ones.append(pair)
        if phase == 0:
            for copy in remote:
                copy.start()
        twos = []
        for p in range(3):
            axis = order[p][phase]
            known = order[p][:phase]
            slot = (phase * 3 + p) * 4 + 2
            pair = []
            for k, sign in enumerate((1, -1)):
                ones[p][k].wait_recv()
                start, width = halves(*PARTS[p])[k]
                came = place(known, axis, (at[axis] - sign + 4) % 4) + (
                    slice(None), pl.ds(start, width),
                )
                copy = push(
                    rows_buf.at[came], rows_buf.at[came], ag_send, ag_recv, slot + k, axis, sign
                )
                copy.start()
                pair.append(copy)
            twos.append(pair)
        for p in range(3):
            for k in range(2):
                ones[p][k].wait_send()
                twos[p][k].wait()

    for copy in local:
        copy.wait()
    for copy in remote:
        copy.wait()

    for y in range(4):
        rows[pl.ds(y * 128, 128), :] = (
            rows_buf[y].astype(F32).reshape(128, ROW).astype(BF16)
        )
    for n in range(4):
        cols = pl.ds(n * 256, 256)
        acc[:, cols] = dot(rows[:, 0:7168], hid_w[:, cols])
    lanes = lax.broadcasted_iota(jnp.int32, (512, 128), 1)
    table = rows[:, 7168:7296].astype(F32)
    hidden = []
    for e in range(2):
        expert = dp * 2 + e
        mine = (lanes == expert) | (lanes == expert + 32)
        weight = jnp.sum(jnp.where(mine, table, 0.0), axis=1, keepdims=True)
        gate_act = acc[:, e * 512:e * 512 + 256]
        up_act = acc[:, e * 512 + 256:e * 512 + 512]
        hidden.append((gate_act / (1.0 + jnp.exp(-gate_act)) * up_act * weight).astype(BF16))
    hidden = jnp.concatenate(hidden, axis=1)

    half_in = ((h0l, h0r), (h1l, h1r), (h2l, h2r))
    full_in = ((f0l, f0r), (f1l, f1r), (f2l, f2r))

    def half_dst(phase, p, k):
        ref = half_in[phase][k]
        _, width = halves(*OUT_PARTS[p])[k]
        return ref.at[(p,) + (slice(None),) * (3 - phase) + (pl.ds(0, width),)]

    def full_dst(phase, p, k):
        ref = full_in[phase][k]
        return ref.at[(p,) + (slice(None),) * (3 - phase) + (pl.ds(0, OUT_PARTS[p][1]),)]

    def first_sends(phase, p):
        axis = order[p][2 - phase]
        known = order[p][:2 - phase]
        pair = []
        for k, sign in enumerate((1, -1)):
            start, width = halves(*OUT_PARTS[p])[k]
            far = place(known, axis, (at[axis] + 2) % 4) + (slice(None), pl.ds(start, width))
            copy = push(
                obuf.at[far], half_dst(phase, p, k), rs_send, rs_recv,
                (phase * 3 + p) * 4 + k, axis, sign,
            )
            copy.start()
            pair.append(copy)
        return pair

    ones = []
    for phase in range(3):
        if phase == 0:
            for p in range(3):
                start, width = OUT_PARTS[p]
                done = 0
                while done < width:
                    size = min(256, width - done)
                    cols = pl.ds(start + done, size)
                    obuf[:, :, :, :, cols] = (
                        dot(hidden, down_w[:, cols]).reshape(4, 4, 4, 8, size).astype(BF16)
                    )
                    done += size
                ones.append(first_sends(0, p))
        else:
            ones = [first_sends(phase, p) for p in range(3)]
        twos = []
        for p in range(3):
            axis = order[p][2 - phase]
            known = order[p][:2 - phase]
            pair = []
            for k, sign in enumerate((1, -1)):
                ones[p][k].wait_recv()
                start, width = halves(*OUT_PARTS[p])[k]
                near = place(known, axis, (at[axis] + sign + 4) % 4)
                part = near + (slice(None), pl.ds(start, width))
                obuf[part] = (
                    obuf[part].astype(F32) + half_dst(phase, p, k)[...].astype(F32)
                ).astype(BF16)
                whole = near + (slice(None), pl.ds(*OUT_PARTS[p]))
                copy = push(
                    obuf.at[whole], full_dst(phase, p, k), rs_send, rs_recv,
                    (phase * 3 + p) * 4 + 2 + k, axis, sign,
                )
                copy.start()
                pair.append(copy)
            twos.append(pair)
        for p in range(3):
            axis = order[p][2 - phase]
            known = order[p][:2 - phase]
            for k in range(2):
                ones[p][k].wait_send()
                twos[p][k].wait()
            start, width = OUT_PARTS[p]
            own = place(known, axis, at[axis]) + (slice(None), pl.ds(start, width))
            total = (
                obuf[own].astype(F32)
                + full_dst(phase, p, 0)[...].astype(F32)
                + full_dst(phase, p, 1)[...].astype(F32)
            )
            if phase < 2:
                obuf[own] = total.astype(BF16)
            else:
                cols = pl.ds(start, width)
                out[:, cols] = (total + stream[:, cols].astype(F32)).astype(BF16)


def per_device(
    cache_pool, send_plan, tables, lengths, new_latent, queries, value_up, out_proj, residual,
    norm_gain, routes, route_weight, gate_proj, up_proj, down_proj,
):
    model = residual.shape[2]
    vmem = pl.BlockSpec(memory_space=pltpu.VMEM)
    smem = pl.BlockSpec(memory_space=pltpu.SMEM)
    hbm = pl.BlockSpec(memory_space=pl.ANY)
    dma = pltpu.SemaphoreType.DMA

    fresh = jnp.transpose(new_latent, (1, 0, 2)).astype(F32)
    resid = residual.reshape(8, model)
    stream, normed = pl.pallas_call(
        attention_kernel,
        out_shape=(
            jax.ShapeDtypeStruct((8, model), BF16),
            jax.ShapeDtypeStruct((8, model), BF16),
        ),
        in_specs=[smem, smem, smem, vmem, vmem, vmem, vmem, hbm, vmem, vmem],
        out_specs=(vmem, vmem),
        scratch_shapes=[
            pltpu.VMEM((32, 576, 128), BF16),
            pltpu.VMEM((32, 576, 128), BF16),
            pltpu.VMEM((576, 1024), BF16),
            pltpu.VMEM((16, 4, 8, LAT), BF16),
            pltpu.VMEM((16, 4, 8, LAT), BF16),
            pltpu.VMEM((512, model), BF16),
            pltpu.VMEM((16, 8, model), BF16),
            pltpu.VMEM((16, 8, model), BF16),
            dma((15,)), dma((15,)), dma((15,)), dma((15,)), dma((15,)), dma((15,)),
            dma((1,)),
        ],
        compiler_params=pltpu.CompilerParams(
            collective_id=0, has_side_effects=True, vmem_limit_bytes=56 * MIB
        ),
        name="attention",
    )(
        send_plan.reshape(-1), tables.reshape(-1), lengths, cache_pool, queries, fresh, value_up,
        out_proj, resid, norm_gain.reshape(1, model),
    )

    matches = routes.reshape(8, 8)[:, :, None] == jnp.arange(32, dtype=jnp.int32)[None, None, :]
    dense = jnp.sum(jnp.where(matches, route_weight.reshape(8, 8)[:, :, None], 0.0), axis=1)
    high = lax.reduce_precision(dense, 8, 7)
    mix = jnp.concatenate([high, dense - high, jnp.zeros((8, 64), F32)], axis=1).astype(BF16)

    def rings(shape, width):
        return [pltpu.VMEM((3,) + shape + (8, width), BF16)] * 2

    scratch = [
        pltpu.VMEM((4, 4, 4, 8, ROW), BF16),
        pltpu.VMEM((512, ROW), BF16),
        pltpu.VMEM((model, 1024), BF16),
        pltpu.VMEM((512, model), BF16),
        pltpu.VMEM((512, 1024), F32),
        pltpu.VMEM((4, 4, 4, 8, model), BF16),
    ]
    for shape in ((4, 4), (4,), ()):
        scratch += rings(shape, 1280)
        scratch += rings(shape, 2432)
    scratch += [dma((36,)), dma((36,)), dma((36,)), dma((36,)), dma((6,)), dma((6,)), dma((6,))]
    result = pl.pallas_call(
        expert_kernel,
        out_shape=jax.ShapeDtypeStruct((8, model), BF16),
        in_specs=[vmem, vmem, vmem, hbm, hbm, hbm],
        out_specs=vmem,
        scratch_shapes=scratch,
        compiler_params=pltpu.CompilerParams(
            collective_id=1, has_side_effects=True, vmem_limit_bytes=60 * MIB
        ),
        name="experts",
    )(normed, mix, stream, gate_proj, up_proj, down_proj)
    return result.reshape(residual.shape)


def solution(mesh):
    placed = (
        P(("dp", "tp"), None, None),
        P(("dp", "tp"), None, None),
        P(("dp", "tp"), None),
        P(("dp", "tp")),
        P(None, ("dp", "tp"), None),
        P(None, ("dp", "tp"), None, None),
        P("dp", None, None),
        P("dp", None),
        P(None, ("dp", "tp"), None),
        P(),
        P(None, ("dp", "tp"), None),
        P(None, ("dp", "tp"), None),
        P("dp", None, "tp"),
        P("dp", None, "tp"),
        P("dp", "tp", None),
    )
    return jax.shard_map(
        per_device,
        mesh=mesh,
        in_specs=placed,
        out_specs=P(None, ("dp", "tp"), None),
        check_vma=False,
    )
```

time: 692 us -> 257 us (0.37); the launches traced: 679 us -> 257 us
  waiting for transfers between devices: 380 us -> 0 us
  Pallas kernels: 0 us -> 249 us
  local copies, waits for them, and re-layouts: 128 us -> 7.24 us
  starting transfers between devices: 62.9 us -> 0 us
  matrix products: 58.8 us -> 0 us
  other arithmetic: 34.1 us -> 0.75 us
  between operations: 14.7 us -> 0.06 us
    all_to_all x7 -> x0, waiting for transfers between devices: 294 us -> none  [the longest x2 111 us: per_device(): lax.all_to_all(spread, ('dp', 'tp'), split_axis=0, concat_axis=0, tiled=T...]
    pallas_call x0 -> x2, Pallas kernels: none -> 249 us  [the longest x1 148 us: per_device(): pl.pallas_call(attention_kernel, out_shape=(jax.ShapeDtypeStruct((8, mode...]
    unnamed x2 -> x0, waiting for transfers between devices: 86.5 us -> none
    all_to_all x7 -> x0, starting transfers between devices: 62.7 us -> none  [the longest x2 21.7 us: per_device(): lax.all_to_all(sendback, ('dp', 'tp'), split_axis=0, concat_axis=0, tiled...]
    reshape x6 -> x4, local copies, waits for them, and re-layouts: 66.6 us -> 5.09 us  [the longest x1 1.6 us: per_device(): return result.reshape(residual.shape)]
    dot_general x18 -> x0, matrix products: 58.8 us -> none  [the longest x2 24.4 us: run_experts(): jnp.einsum('erh,ehd->erd', hidden, down_proj, preferred_element_type=jnp....]
    reduce_sum x12 -> x1, other arithmetic: 22.8 us -> 0.09 us  [per_device(): jnp.sum(jnp.where(matches, route_weight.reshape(8, 8)[:, :, None], 0.0),...]
    another operation x3 -> x0, local copies, waits for them, and re-layouts: 16.4 us -> none  [the longest x2 16.4 us: per_device(): jnp.transpose(lane_major, (1, 0, 2, 3, 4))]
  transfers between devices with their start and end apart: 8 -> 0, of which waited for: 8 -> 0; matrix products, arithmetic and copies ran while one was open for 22% -> 0% of each run, Pallas kernels for 0% -> 0%
where the time goes in v1:
time: 257 us
  Pallas kernels  249 us (97%)
  local copies, waits for them, and re-layouts  7.24 us (3%)
    pallas_call x1, Pallas kernels, per_device(): pl.pallas_call(attention_kernel, out_shape=(jax.ShapeDtypeStruct((8, mode...  148 us
    pallas_call x1, Pallas kernels, per_device(): pl.pallas_call(expert_kernel, out_shape=jax.ShapeDtypeStruct((8, model),...  101 us

profile of v1, /device:TPU:0, one launch (start us, length us, event | category | flops | bytes accessed | tf_op | source)
XLA Modules:
  0.0 256.8 jit_solution(12233322752213035816)
XLA Ops:
  0.0 0.8 copy.22
  0.8 0.6 reshape.17.plan
  1.3 1.4 reshape.18.tab
  2.7 1.3 copy.25
  4.0 1.6 reshape.19.resid
  5.6 0.0 copy-start
  5.6 0.0 copy-start.1
  5.6 147.5 %attention.1 = (bf16[8,7168]{1,0:T(8,128)(2,1)}, bf16[8,7168]{1,0:T(8,128)(2,1)}) custom-call(s32[32]{0:T(128)} %reshape.17.plan, s32[32]{0:T(128)} %reshape.18.tab, s32[4]{0:T(128)} %lens.1, bf16[24,576,128]{2,1,0:T(8,128)(2,1)} %pool.1, bf16[2,4,64,576]{3,2,1,0:T(8,128)(2,1)} %queries.1, f32[4,2,576]{2,1,0:T(2,128)} %bitcast.6, ...), custom_call_target="tpu_custom_call" | custom-call | tf_op jit(solution)/shard_map/attention/pallas_call | solution.py:423
  153.1 0.0 copy-done
  153.1 0.0 copy-done.1
  153.1 0.1 select_reduce_fusion
  153.2 0.1 pad.2.clone
  153.3 0.7 maximum_maximum_fusion.mix
  154.0 101.2 %experts.1 = bf16[8,7168]{1,0:T(8,128)(2,1)} custom-call(bf16[8,7168]{1,0:T(8,128)(2,1)} %get-tuple-element.7.normed, bf16[8,128]{1,0:T(8,128)(2,1)} %maximum_maximum_fusion.mix, bf16[8,7168]{1,0:T(8,128)(2,1)} %get-tuple-element.8.stream, bf16[2,7168,128]{2,1,0:T(8,128)(2,1)} %gate.1, bf16[2,7168,128]{2,1,0:T(8,128)(2,1)} %up.1, bf16[2,128,7168]{2,1,0:T(8,128)(2,1)} %down.1), custom_call_target="tpu_custom_call" | custom-call | tf_op jit(solution)/shard_map/experts/pallas_call | solution.py:472
  255.2 1.6 reshape.21
  (2 shorter events, 0.0 us)
Async XLA Ops:
  5.6 147.5 %copy-start = (f32[2,4,8]{2,1,0:T(4,128)S(1)}, f32[2,4,8]{2,1,0:T(4,128)}, u32[]{:S(2)}) copy-start(f32[2,4,8]{2,1,0:T(4,128)} %param.26) | copy-start | bytes 772
  5.6 147.5 %copy-start.1 = (s32[2,4,8]{2,1,0:T(4,128)S(1)}, s32[2,4,8]{2,1,0:T(4,128)}, u32[]{:S(2)}) copy-start(s32[2,4,8]{2,1,0:T(4,128)} %param.25) | copy-start | bytes 772

commit v2 on v1

--- a/solution.py
+++ b/solution.py
@@ -24,19 +24,116 @@
     return lax.dot_general(a, b, (((1,), (1,)), ((), ())), preferred_element_type=F32)
 
 
+def halves(start, width):
+    tiles = width // 128
+    first = (tiles + 1) // 2 * 128
+    return (start, first), (start + first, width - first)
+
+
+def ring_sum(at, orders, parts, buf, half_in, full_in, sends, recvs, neighbour, produce, finish):
+    axes = len(orders[0])
+    count = len(parts)
+
+    def place(reduced, axis, value):
+        where = [slice(None)] * axes
+        for a in reduced:
+            where[a] = at[a]
+        where[axis] = value
+        return tuple(where)
+
+    def landing(refs, phase, p, k, width):
+        return refs[phase][k].at[(p,) + (slice(None),) * (axes - phase) + (pl.ds(0, width),)]
+
+    def push(src, dst, slot, axis, sign):
+        copy = pltpu.make_async_remote_copy(
+            src_ref=src,
+            dst_ref=dst,
+            send_sem=sends.at[slot],
+            recv_sem=recvs.at[slot],
+            device_id=neighbour(axis, sign),
+            device_id_type=MESH,
+        )
+        copy.start()
+        return copy
+
+    for phase in range(axes):
+        ones = []
+        for p in range(count):
+            if phase == 0:
+                produce(p)
+            axis, reduced = orders[p][phase], orders[p][:phase]
+            pair = []
+            for k, sign in enumerate((1, -1)):
+                start, width = halves(*parts[p])[k]
+                far = place(reduced, axis, (at[axis] + 2) % 4) + (slice(None), pl.ds(start, width))
+                pair.append(
+                    push(
+                        buf.at[far], landing(half_in, phase, p, k, width),
+                        (phase * count + p) * 4 + k, axis, sign,
+                    )
+                )
+            ones.append(pair)
+        twos = []
+        for p in range(count):
+            axis, reduced = orders[p][phase], orders[p][:phase]
+            pair = []
+            for k, sign in enumerate((1, -1)):
+                ones[p][k].wait_recv()
+                start, width = halves(*parts[p])[k]
+                near = place(reduced, axis, (at[axis] + sign + 4) % 4)
+                half = near + (slice(None), pl.ds(start, width))
+                buf[half] = (
+                    buf[half].astype(F32) + landing(half_in, phase, p, k, width)[...].astype(F32)
+                ).astype(BF16)
+                whole = near + (slice(None), pl.ds(*parts[p]))
+                pair.append(
+                    push(
+                        buf.at[whole], landing(full_in, phase, p, k, parts[p][1]),
+                        (phase * count + p) * 4 + 2 + k, axis, sign,
+                    )
+                )
+            twos.append(pair)
+        for p in range(count):
+            axis, reduced = orders[p][phase], orders[p][:phase]
+            for k in range(2):
+                ones[p][k].wait_send()
+                twos[p][k].wait()
+            start, width = parts[p]
+            own = place(reduced, axis, at[axis]) + (slice(None), pl.ds(start, width))
+            total = (
+                buf[own].astype(F32)
+                + landing(full_in, phase, p, 0, width)[...].astype(F32)
+                + landing(full_in, phase, p, 1, width)[...].astype(F32)
+            )
+            if phase < axes - 1:
+                buf[own] = total.astype(BF16)
+            else:
+                finish(p, pl.ds(start, width), total)
+
+
+PROJ_PARTS = ((0, 3584), (3584, 3584))
+
+
 def attention_kernel(
-    plan, tab, lens, pool, queries, fresh, value_up, proj_hbm, resid, gain,
+    plan, tab, lens, pool, queries, new_latent, value_up, proj_hbm, resid, gain,
     stream_out, normed_out,
-    outgoing, arrived, keys, lat_send, lat_recv, proj, part_send, part_recv,
-    mig_send, mig_recv, lat_s, lat_r, part_s, part_r, local_sem,
+    outgoing, middle, near_fwd, far_fwd, arrived, keys, fresh, lat_send, lat_recv, proj, part,
+    wide_sum, h0l, h0r, f0l, f0r, h1l, h1r, f1l, f1r,
+    mig_s, mig_r, lat_s, lat_r, part_s, part_r, local_sem,
 ):
     groups = 16
     me = lax.axis_index("dp")
     lane = lax.axis_index("tp")
+    at = (me // 4, me % 4)
     model = proj_hbm.shape[1]
 
     proj_copy = pltpu.make_async_copy(proj_hbm, proj, local_sem.at[0])
     proj_copy.start()
+
+    def neighbour(axis, sign):
+        new = list(at)
+        new[axis] = (at[axis] + sign + 4) % 4
+        return (new[0] * 4 + new[1], lane)
 
     barrier = pltpu.get_barrier_semaphore()
     for shift in range(1, groups):
@@ -44,12 +141,69 @@
             barrier, inc=1, device_id=(lax.rem(me + shift, groups), lane), device_id_type=MESH
         )
 
-    def pick(i, carry):
-        outgoing[i] = pool[jnp.maximum(plan[i], 0)]
-        return carry
-
-    lax.fori_loop(0, 2 * groups, pick, 0)
+    for c in range(2):
+        def pick(i, carry):
+            outgoing[c, i // 4, i % 4] = pool[jnp.maximum(plan[0, i, c], 0)]
+            return carry
+
+        lax.fori_loop(0, groups, pick, 0)
+    for k in range(2):
+        fresh[k] = new_latent[k].astype(F32)
     pl.semaphore_wait(barrier, groups - 1)
+
+    def push(src, dst, slot, axis, sign):
+        copy = pltpu.make_async_remote_copy(
+            src_ref=src,
+            dst_ref=dst,
+            send_sem=mig_s.at[slot],
+            recv_sem=mig_r.at[slot],
+            device_id=neighbour(axis, sign),
+            device_id_type=MESH,
+        )
+        copy.start()
+        return copy
+
+    def pair_at(axis, value, k):
+        rest = pl.ds(0, 4) if k is None else pl.ds(2 * k, 2)
+        return (rest, value) if axis == 1 else (value, rest)
+
+    def local(src, dst, n):
+        copy = pltpu.make_async_copy(src, dst, local_sem.at[n])
+        copy.start()
+        return copy
+
+    for stage in range(2):
+        source, target = (outgoing, middle) if stage == 0 else (middle, arrived)
+        fwd = (near_fwd, far_fwd)[stage]
+        first, kept = [], []
+        for c in range(2):
+            axis = 1 - c if stage == 0 else c
+            far = (at[axis] + 2) % 4
+            for k, sign in enumerate((1, -1)):
+                base = ((stage * 2 + c) * 2 + k) * 3
+                halfway = push(
+                    source.at[(c,) + pair_at(axis, far, k)], fwd.at[c, k], base, axis, sign
+                )
+                beside = push(
+                    source.at[(c,) + pair_at(axis, (at[axis] + sign + 4) % 4, None)],
+                    target.at[(c,) + pair_at(axis, at[axis], None)],
+                    base + 1, axis, sign,
+                )
+                first.append((c, k, sign, axis, base, halfway, beside))
+            own = (c,) + pair_at(axis, at[axis], None)
+            kept.append(local(source.at[own], target.at[own], 1 + stage * 2 + c))
+        second = []
+        for c, k, sign, axis, base, halfway, beside in first:
+            halfway.wait_recv()
+            came = (at[axis] - sign + 4) % 4
+            second.append(
+                push(fwd.at[c, k], target.at[(c,) + pair_at(axis, came, k)], base + 2, axis, sign)
+            )
+        for c, k, sign, axis, base, halfway, beside in first:
+            halfway.wait_send()
+            beside.wait()
+        for copy in second + kept:
+            copy.wait()
 
     def exchange(src, dst, send_sem, recv_sem, shift):
         peer = lax.rem(me + shift, groups)
@@ -62,21 +216,6 @@
             device_id_type=MESH,
         )
 
-    moves = [
-        exchange(
-            lambda p: outgoing.at[pl.ds(2 * p, 2)],
-            lambda m: arrived.at[pl.ds(2 * m, 2)],
-            mig_send, mig_recv, shift,
-        )
-        for shift in range(1, groups)
-    ]
-    for move in moves:
-        move.start()
-    arrived[2 * me] = outgoing[2 * me]
-    arrived[2 * me + 1] = outgoing[2 * me + 1]
-    for move in moves:
-        move.wait()
-
     row = lax.broadcasted_iota(jnp.int32, (128, 128), 0)
     col = lax.broadcasted_iota(jnp.int32, (128, 128), 1)
     reorder = jnp.where(
@@ -87,18 +226,20 @@
 
     def attend(s, carry):
         for j in range(8):
-            entry = tab[s * 8 + j]
+            entry = tab[s, j]
             own = pool[jnp.minimum(entry, 23)]
-            moved = arrived[jnp.maximum(entry - 24, 0)]
+            came = jnp.maximum(entry - 24, 0)
+            moved = arrived[came & 1, came >> 3, (came >> 1) & 3]
             keys[:, j * 128:(j + 1) * 128] = jnp.where(entry < 24, own, moved)
         q = jnp.concatenate([queries[0, s], queries[1, s]], axis=0)
         q = dot(reorder, q)
         q16 = q.astype(BF16)
         scores = dot(q16, keys[...]) * SCALE
         scores = jnp.where(position < lens[s], scores, -jnp.inf)
-        new = fresh[s]
-        first = jnp.sum(q * new[0:1], axis=1, keepdims=True) * SCALE
-        second = jnp.sum(q * new[1:2], axis=1, keepdims=True) * SCALE
+        new0 = fresh[0, pl.ds(s, 1), :]
+        new1 = fresh[1, pl.ds(s, 1), :]
+        first = jnp.sum(q * new0, axis=1, keepdims=True) * SCALE
+        second = jnp.sum(q * new1, axis=1, keepdims=True) * SCALE
         second = jnp.where(second_step, second, -jnp.inf)
         largest = jnp.maximum(jnp.max(scores, axis=1, keepdims=True), jnp.maximum(first, second))
         weights = jnp.exp(scores - largest)
@@ -109,7 +250,7 @@
         first = (first / total).astype(BF16).astype(F32)
         second = (second / total).astype(BF16).astype(F32)
         latent = dot_nt(probs, keys[0:LAT, :])
-        latent = latent + first * new[0:1, 0:LAT] + second * new[1:2, 0:LAT]
+        latent = latent + first * new0[:, 0:LAT] + second * new1[:, 0:LAT]
         lat_send[:, pl.ds(s, 1)] = latent.reshape(16, 1, 8, LAT).astype(BF16)
         return carry
 
@@ -136,25 +277,29 @@
         heads.append(dot(take, up).astype(BF16))
     heads = jnp.concatenate(heads, axis=1)
     proj_copy.wait()
+
+    def produce(p):
+        start, width = PROJ_PARTS[p]
+        chunk = 896
+        for n in range(width // chunk):
+            cols = pl.ds(start + n * chunk, chunk)
+            part[:, :, :, cols] = dot(heads, proj[:, cols]).reshape(4, 4, 8, chunk).astype(BF16)
+
+    def finish(p, cols, total):
+        wide_sum[:, cols] = total
+
+    ring_sum(
+        at, ((1, 0), (0, 1)), PROJ_PARTS, part, ((h0l, h0r), (h1l, h1r)),
+        ((f0l, f0r), (f1l, f1r)), part_s, part_r, neighbour, produce, finish,
+    )
+
     chunk = 1024
-    for n in range(model // chunk):
-        cols = pl.ds(n * chunk, chunk)
-        part_send[:, :, cols] = dot(heads, proj[:, cols]).reshape(16, 8, chunk).astype(BF16)
-
-    moves = [
-        exchange(lambda p: part_send.at[p], lambda m: part_recv.at[m], part_s, part_r, shift)
-        for shift in range(1, groups)
-    ]
-    for move in moves:
-        move.start()
-    part_recv[me] = part_send[me]
-    for move in moves:
-        move.wait()
-
     square = jnp.zeros((8, 1), F32)
     for n in range(model // chunk):
         cols = pl.ds(n * chunk, chunk)
-        total = resid[:, cols].astype(F32) + jnp.sum(part_recv[:, :, cols].astype(F32), axis=0)
+        total = wide_sum[:, cols] + jnp.concatenate(
+            [resid[0, :, cols].astype(F32), resid[1, :, cols].astype(F32)], axis=0
+        )
         stream = total.astype(BF16)
         stream_out[:, cols] = stream
         wide = stream.astype(F32)
@@ -169,12 +314,6 @@
 PARTS = ((0, 2432), (2432, 2432), (4864, 2432))
 OUT_PARTS = ((0, 2432), (2432, 2432), (4864, 2304))
 ROW = 7296
-
-
-def halves(start, width):
-    tiles = width // 128
-    first = (tiles + 1) // 2 * 128
-    return (start, first), (start + first, width - first)
 
 
 def expert_kernel(
@@ -324,88 +463,26 @@
         hidden.append((gate_act / (1.0 + jnp.exp(-gate_act)) * up_act * weight).astype(BF16))
     hidden = jnp.concatenate(hidden, axis=1)
 
-    half_in = ((h0l, h0r), (h1l, h1r), (h2l, h2r))
-    full_in = ((f0l, f0r), (f1l, f1r), (f2l, f2r))
-
-    def half_dst(phase, p, k):
-        ref = half_in[phase][k]
-        _, width = halves(*OUT_PARTS[p])[k]
-        return ref.at[(p,) + (slice(None),) * (3 - phase) + (pl.ds(0, width),)]
-
-    def full_dst(phase, p, k):
-        ref = full_in[phase][k]
-        return ref.at[(p,) + (slice(None),) * (3 - phase) + (pl.ds(0, OUT_PARTS[p][1]),)]
-
-    def first_sends(phase, p):
-        axis = order[p][2 - phase]
-        known = order[p][:2 - phase]
-        pair = []
-        for k, sign in enumerate((1, -1)):
-            start, width = halves(*OUT_PARTS[p])[k]
-            far = place(known, axis, (at[axis] + 2) % 4) + (slice(None), pl.ds(start, width))
-            copy = push(
-                obuf.at[far], half_dst(phase, p, k), rs_send, rs_recv,
-                (phase * 3 + p) * 4 + k, axis, sign,
+    def produce(p):
+        start, width = OUT_PARTS[p]
+        done = 0
+        while done < width:
+            size = min(256, width - done)
+            cols = pl.ds(start + done, size)
+            obuf[:, :, :, :, cols] = (
+                dot(hidden, down_w[:, cols]).reshape(4, 4, 4, 8, size).astype(BF16)
             )
-            copy.start()
-            pair.append(copy)
-        return pair
-
-    ones = []
-    for phase in range(3):
-        if phase == 0:
-            for p in range(3):
-                start, width = OUT_PARTS[p]
-                done = 0
-                while done < width:
-                    size = min(256, width - done)
-                    cols = pl.ds(start + done, size)
-                    obuf[:, :, :, :, cols] = (
-                        dot(hidden, down_w[:, cols]).reshape(4, 4, 4, 8, size).astype(BF16)
-                    )
-                    done += size
-                ones.append(first_sends(0, p))
-        else:
-            ones = [first_sends(phase, p) for p in range(3)]
-        twos = []
-        for p in range(3):
-            axis = order[p][2 - phase]
-            known = order[p][:2 - phase]
-            pair = []
-            for k, sign in enumerate((1, -1)):
-                ones[p][k].wait_recv()
-                start, width = halves(*OUT_PARTS[p])[k]
-                near = place(known, axis, (at[axis] + sign + 4) % 4)
-                part = near + (slice(None), pl.ds(start, width))
-                obuf[part] = (
-                    obuf[part].astype(F32) + half_dst(phase, p, k)[...].astype(F32)
-                ).astype(BF16)
-                whole = near + (slice(None), pl.ds(*OUT_PARTS[p]))
-                copy = push(
-                    obuf.at[whole], full_dst(phase, p, k), rs_send, rs_recv,
-                    (phase * 3 + p) * 4 + 2 + k, axis, sign,
-                )
-                copy.start()
-                pair.append(copy)
-            twos.append(pair)
-        for p in range(3):
-            axis = order[p][2 - phase]
-            known = order[p][:2 - phase]
-            for k in range(2):
-                ones[p][k].wait_send()
-                twos[p][k].wait()
-            start, width = OUT_PARTS[p]
-            own = place(known, axis, at[axis]) + (slice(None), pl.ds(start, width))
-            total = (
-                obuf[own].astype(F32)
-                + full_dst(phase, p, 0)[...].astype(F32)
-                + full_dst(phase, p, 1)[...].astype(F32)
-            )
-            if phase < 2:
-                obuf[own] = total.astype(BF16)
-            else:
-                cols = pl.ds(start, width)
-                out[:, cols] = (total + stream[:, cols].astype(F32)).astype(BF16)
+            done += size
+
+    def finish(p, cols, total):
+        total = total + stream[:, cols].astype(F32)
+        out[0, :, cols] = total[0:4].astype(BF16)
+        out[1, :, cols] = total[4:8].astype(BF16)
+
+    ring_sum(
+        at, [o[::-1] for o in order], OUT_PARTS, obuf, ((h0l, h0r), (h1l, h1r), (h2l, h2r)),
+        ((f0l, f0r), (f1l, f1r), (f2l, f2r)), rs_send, rs_recv, neighbour, produce, finish,
+    )
 
 
 def per_device(
@@ -418,8 +495,28 @@
     hbm = pl.BlockSpec(memory_space=pl.ANY)
     dma = pltpu.SemaphoreType.DMA
 
-    fresh = jnp.transpose(new_latent, (1, 0, 2)).astype(F32)
-    resid = residual.reshape(8, model)
+
+    def rings(parts, shape, width):
+        return [pltpu.VMEM((parts,) + shape + (8, width), BF16)] * 2
+
+    scratch = [
+        pltpu.VMEM((2, 4, 4, 576, 128), BF16),
+        pltpu.VMEM((2, 4, 4, 576, 128), BF16),
+        pltpu.VMEM((2, 2, 2, 576, 128), BF16),
+        pltpu.VMEM((2, 2, 2, 576, 128), BF16),
+        pltpu.VMEM((2, 4, 4, 576, 128), BF16),
+        pltpu.VMEM((576, 1024), BF16),
+        pltpu.VMEM((2, 4, 576), F32),
+        pltpu.VMEM((16, 4, 8, LAT), BF16),
+        pltpu.VMEM((16, 4, 8, LAT), BF16),
+        pltpu.VMEM((512, model), BF16),
+        pltpu.VMEM((4, 4, 8, model), BF16),
+        pltpu.VMEM((8, model), F32),
+    ]
+    for shape in ((4,), ()):
+        scratch += rings(2, shape, 1792)
+        scratch += rings(2, shape, 3584)
+    scratch += [dma((24,)), dma((24,)), dma((15,)), dma((15,)), dma((16,)), dma((16,)), dma((5,))]
     stream, normed = pl.pallas_call(
         attention_kernel,
         out_shape=(
@@ -428,34 +525,20 @@
         ),
         in_specs=[smem, smem, smem, vmem, vmem, vmem, vmem, hbm, vmem, vmem],
         out_specs=(vmem, vmem),
-        scratch_shapes=[
-            pltpu.VMEM((32, 576, 128), BF16),
-            pltpu.VMEM((32, 576, 128), BF16),
-            pltpu.VMEM((576, 1024), BF16),
-            pltpu.VMEM((16, 4, 8, LAT), BF16),
-            pltpu.VMEM((16, 4, 8, LAT), BF16),
-            pltpu.VMEM((512, model), BF16),
-            pltpu.VMEM((16, 8, model), BF16),
-            pltpu.VMEM((16, 8, model), BF16),
-            dma((15,)), dma((15,)), dma((15,)), dma((15,)), dma((15,)), dma((15,)),
-            dma((1,)),
-        ],
+        scratch_shapes=scratch,
         compiler_params=pltpu.CompilerParams(
             collective_id=0, has_side_effects=True, vmem_limit_bytes=56 * MIB
         ),
         name="attention",
     )(
-        send_plan.reshape(-1), tables.reshape(-1), lengths, cache_pool, queries, fresh, value_up,
-        out_proj, resid, norm_gain.reshape(1, model),
+        send_plan, tables, lengths, cache_pool, queries, new_latent, value_up,
+        out_proj, residual, norm_gain.reshape(1, model),
     )
 
     matches = routes.reshape(8, 8)[:, :, None] == jnp.arange(32, dtype=jnp.int32)[None, None, :]
     dense = jnp.sum(jnp.where(matches, route_weight.reshape(8, 8)[:, :, None], 0.0), axis=1)
     high = lax.reduce_precision(dense, 8, 7)
     mix = jnp.concatenate([high, dense - high, jnp.zeros((8, 64), F32)], axis=1).astype(BF16)
-
-    def rings(shape, width):
-        return [pltpu.VMEM((3,) + shape + (8, width), BF16)] * 2
 
     scratch = [
         pltpu.VMEM((4, 4, 4, 8, ROW), BF16),
@@ -466,12 +549,12 @@
         pltpu.VMEM((4, 4, 4, 8, model), BF16),
     ]
     for shape in ((4, 4), (4,), ()):
-        scratch += rings(shape, 1280)
-        scratch += rings(shape, 2432)
+        scratch += rings(3, shape, 1280)
+        scratch += rings(3, shape, 2432)
     scratch += [dma((36,)), dma((36,)), dma((36,)), dma((36,)), dma((6,)), dma((6,)), dma((6,))]
     result = pl.pallas_call(
         expert_kernel,
-        out_shape=jax.ShapeDtypeStruct((8, model), BF16),
+        out_shape=jax.ShapeDtypeStruct(residual.shape, BF16),
         in_specs=[vmem, vmem, vmem, hbm, hbm, hbm],
         out_specs=vmem,
         scratch_shapes=scratch,
@@ -480,7 +563,7 @@
         ),
         name="experts",
     )(normed, mix, stream, gate_proj, up_proj, down_proj)
-    return result.reshape(residual.shape)
+    return result
 
 
 def solution(mesh):

time: 257 us -> 199 us (0.77)
  Pallas kernels: 249 us -> 194 us
  local copies, waits for them, and re-layouts: 7.24 us -> 3.02 us
    pallas_call x1, Pallas kernels: 148 us -> 100 us  [per_device(): pl.pallas_call(attention_kernel, out_shape=(jax.ShapeDtypeStruct((8, mode...]
    pallas_call x1, Pallas kernels: 101 us -> 94.3 us  [per_device(): pl.pallas_call(expert_kernel, out_shape=jax.ShapeDtypeStruct(residual.sha...]
    reshape x4 -> x0, local copies, waits for them, and re-layouts: 5.09 us -> none  [the longest x1 1.6 us: per_device(): return result.reshape(residual.shape)]
where the time goes in v2:
time: 199 us
  Pallas kernels  194 us (97%)
  local copies, waits for them, and re-layouts  3.02 us (2%)
    pallas_call x1, Pallas kernels, per_device(): pl.pallas_call(attention_kernel, out_shape=(jax.ShapeDtypeStruct((8, mode...  100 us
    pallas_call x1, Pallas kernels, per_device(): pl.pallas_call(expert_kernel, out_shape=jax.ShapeDtypeStruct(residual.sha...  94.3 us

profile of v2, /device:TPU:0, one launch (start us, length us, event | category | flops | bytes accessed | tf_op | source)
XLA Modules:
  0.0 199.0 jit_solution(10331879070532604199)
XLA Ops:
  0.0 0.1 pad.2.clone
  0.1 0.8 select_reduce_fusion
  0.9 0.7 maximum_maximum_fusion.mix
  1.6 1.4 copy.17.plan
  2.9 100.2 %attention.1 = (bf16[8,7168]{1,0:T(8,128)(2,1)}, bf16[8,7168]{1,0:T(8,128)(2,1)}) custom-call(s32[1,16,2]{2,1,0:T(8,128)} %copy.17.plan, s32[4,8]{1,0:T(4,128)} %tab.1, s32[4]{0:T(128)} %lens.1, bf16[24,576,128]{2,1,0:T(8,128)(2,1)} %pool.1, bf16[2,4,64,576]{3,2,1,0:T(8,128)(2,1)} %queries.1, bf16[2,4,576]{2,1,0:T(4,128)(2,1)} %new_latent.1, ...), custom_call_target="tpu_custom_call" | custom-call | tf_op jit(solution)/shard_map/attention/pallas_call | solution.py:520
  103.1 94.3 %experts.1 = bf16[2,4,7168]{2,1,0:T(4,128)(2,1)} custom-call(bf16[8,7168]{1,0:T(8,128)(2,1)} %get-tuple-element.7.normed, bf16[8,128]{1,0:T(8,128)(2,1)} %maximum_maximum_fusion.mix, bf16[8,7168]{1,0:T(8,128)(2,1)} %get-tuple-element.8.stream, bf16[2,7168,128]{2,1,0:T(8,128)(2,1)} %gate.1, bf16[2,7168,128]{2,1,0:T(8,128)(2,1)} %up.1, bf16[2,128,7168]{2,1,0:T(8,128)(2,1)} %down.1), custom_call_target="tpu_custom_call" | custom-call | tf_op jit(solution)/shard_map/experts/pallas_call | solution.py:555
  197.4 1.6 copy.19
  (2 shorter events, 0.0 us)

commit v3 on v2

--- a/solution.py
+++ b/solution.py
@@ -319,14 +319,17 @@
 def expert_kernel(
     normed, mix, stream, gate, up, down,
     out,
-    rows_buf, rows, hid_w, down_w, acc, obuf,
+    rows, hid_w, down_w, acc, obuf,
     h0l, h0r, f0l, f0r, h1l, h1r, f1l, f1r, h2l, h2r, f2l, f2r,
-    ag_send, ag_recv, rs_send, rs_recv, w_send, w_recv, w_local,
+    g0_send, g0_recv, g1_send, g1_recv, g2_send, g2_recv,
+    s0_send, s0_recv, s1_send, s1_recv, s2_send, s2_recv, w_send, w_recv, w_local,
 ):
     dp = lax.axis_index("dp")
     tp = lax.axis_index("tp")
     at = (dp // 4, dp % 4, tp // 2)
     core = tp % 2
+    signs = (1, -1)
+    every = slice(None)
 
     def neighbour(axis, sign):
         new = list(at)
@@ -337,28 +340,22 @@
 
     barrier = pltpu.get_barrier_semaphore()
     for axis in range(3):
-        for sign in (1, -1):
+        for sign in signs:
             pl.semaphore_signal(
                 barrier, inc=1, device_id=neighbour(axis, sign), device_id_type=MESH
             )
     pl.semaphore_signal(barrier, inc=1, device_id=partner, device_id_type=MESH)
 
-    rows_buf[at[0], at[1], at[2], :, 0:7168] = normed[...]
-    rows_buf[at[0], at[1], at[2], :, 7168:7296] = mix[...]
+    rows[at[0], at[1], at[2], :, 0:7168] = normed[...]
+    rows[at[0], at[1], at[2], :, 7168:7296] = mix[...]
     local = []
     remote = []
 
     def spots(e, which):
         if which < 2:
             base = e * 512 + which * 256
-            return (
-                hid_w.at[:, pl.ds(base, 128)],
-                hid_w.at[:, pl.ds(base + 128, 128)],
-            )
-        return (
-            down_w.at[pl.ds(e * 256, 128)],
-            down_w.at[pl.ds(e * 256 + 128, 128)],
-        )
+            return hid_w.at[:, pl.ds(base, 128)], hid_w.at[:, pl.ds(base + 128, 128)]
+        return down_w.at[pl.ds(e * 256, 128)], down_w.at[pl.ds(e * 256 + 128, 128)]
 
     for e in range(2):
         for which, ref in enumerate((gate, up, down)):
@@ -381,89 +378,195 @@
 
     order = [(p, (p + 1) % 3, (p + 2) % 3) for p in range(3)]
 
-    def place(known, axis, value):
-        where = [at[0], at[1], at[2]]
-        for a in known:
-            where[a] = slice(None)
-        where[axis] = value
-        return tuple(where)
-
-    def push(ref, dst, sends, recvs, slot, axis, sign):
-        return pltpu.make_async_remote_copy(
-            src_ref=ref,
+    def shifted(axis, offset):
+        return (at[axis] + offset + 4) % 4
+
+    def block(p, values, start, width):
+        where = [None] * 3
+        for axis, value in zip(order[p], values):
+            where[axis] = every if value is None else value
+        return tuple(where) + (every, pl.ds(start, width))
+
+    def push(src, dst, sends, recvs, slot, axis, sign):
+        copy = pltpu.make_async_remote_copy(
+            src_ref=src,
             dst_ref=dst,
             send_sem=sends.at[slot],
             recv_sem=recvs.at[slot],
             device_id=neighbour(axis, sign),
             device_id_type=MESH,
         )
-
-    for phase in range(3):
-        ones = []
+        copy.start()
+        return copy
+
+    def both(p, values, axis, sems, slot):
+        ref = rows.at[block(p, values, *PARTS[p])]
+        return [push(ref, ref, *sems, slot + k, axis, sign) for k, sign in enumerate(signs)]
+
+    def forward(p, k, came, axis, sems, slot):
+        ref = rows.at[block(p, came, *halves(*PARTS[p])[k])]
+        return push(ref, ref, *sems, slot + 2 + k, axis, signs[k])
+
+    sems0, sems1, sems2 = (g0_send, g0_recv), (g1_send, g1_recv), (g2_send, g2_recv)
+    one, two = {}, {}
+
+    def start_unit(p, d):
+        a, b, c = order[p]
+        one[2, p, d] = both(p, (None, shifted(b, d), at[c]), c, sems2, (p * 4 + d) * 4)
+
+    def forward_unit(p, d):
+        a, b, c = order[p]
+        two[2, p, d] = []
+        for k in range(2):
+            one[2, p, d][k].wait_recv()
+            two[2, p, d].append(
+                forward(
+                    p, k, (None, shifted(b, d), shifted(c, -signs[k])), c, sems2, (p * 4 + d) * 4
+                )
+            )
+
+    for p in range(3):
+        a, b, c = order[p]
+        one[0, p] = both(p, (at[a], at[b], at[c]), a, sems0, p * 4)
+    for copy in remote:
+        copy.start()
+    for p in range(3):
+        a, b, c = order[p]
+        two[0, p] = []
+        for k in range(2):
+            one[0, p][k].wait_recv()
+            two[0, p].append(
+                forward(p, k, (shifted(a, -signs[k]), at[b], at[c]), a, sems0, p * 4)
+            )
+    for p in range(3):
+        a, b, c = order[p]
+        for copy in two[0, p]:
+            copy.wait_recv()
+        one[1, p] = both(p, (None, at[b], at[c]), b, sems1, p * 4)
+        start_unit(p, 0)
+    for p in range(3):
+        a, b, c = order[p]
+        two[1, p] = []
+        for k in range(2):
+            one[1, p][k].wait_recv()
+            two[1, p].append(
+                forward(p, k, (None, shifted(b, -signs[k]), at[c]), b, sems1, p * 4)
+            )
+        start_unit(p, 3)
+        start_unit(p, 1)
+    for p in range(3):
+        forward_unit(p, 0)
+    for p in range(3):
+        for copy in two[1, p]:
+            copy.wait_recv()
+        start_unit(p, 2)
+    for d in (3, 1):
         for p in range(3):
-            axis = order[p][phase]
-            known = order[p][:phase]
-            start, width = PARTS[p]
-            own = place(known, axis, at[axis]) + (slice(None), pl.ds(start, width))
-            slot = (phase * 3 + p) * 4
-            pair = [
-                push(rows_buf.at[own], rows_buf.at[own], ag_send, ag_recv, slot + k, axis, sign)
-                for k, sign in enumerate((1, -1))
-            ]
-            for copy in pair:
-                copy.start()
-            ones.append(pair)
-        if phase == 0:
-            for copy in remote:
-                copy.start()
-        twos = []
-        for p in range(3):
-            axis = order[p][phase]
-            known = order[p][:phase]
-            slot = (phase * 3 + p) * 4 + 2
-            pair = []
-            for k, sign in enumerate((1, -1)):
-                ones[p][k].wait_recv()
-                start, width = halves(*PARTS[p])[k]
-                came = place(known, axis, (at[axis] - sign + 4) % 4) + (
-                    slice(None), pl.ds(start, width),
-                )
-                copy = push(
-                    rows_buf.at[came], rows_buf.at[came], ag_send, ag_recv, slot + k, axis, sign
-                )
-                copy.start()
-                pair.append(copy)
-            twos.append(pair)
-        for p in range(3):
-            for k in range(2):
-                ones[p][k].wait_send()
-                twos[p][k].wait()
-
+            forward_unit(p, d)
+
+    acc[...] = jnp.zeros_like(acc)
     for copy in local:
         copy.wait()
     for copy in remote:
         copy.wait()
 
-    for y in range(4):
-        rows[pl.ds(y * 128, 128), :] = (
-            rows_buf[y].astype(F32).reshape(128, ROW).astype(BF16)
-        )
-    for n in range(4):
-        cols = pl.ds(n * 256, 256)
-        acc[:, cols] = dot(rows[:, 0:7168], hid_w[:, cols])
+    def multiply(p, d):
+        a, b, c = order[p]
+        for copy in two[2, p, d]:
+            copy.wait_recv()
+        start, width = OUT_PARTS[p]
+        lhs = rows[block(p, (None, shifted(b, d), None), start, width)]
+        lhs = lhs.astype(F32).reshape(128, width).astype(BF16)
+        for n in range(4):
+            cols = (n * 256, 256)
+            where = block(p, (None, shifted(b, d), None), *cols)
+            product = dot(lhs, hid_w[pl.ds(start, width), pl.ds(*cols)])
+            acc[where] = acc[where] + product.reshape(4, 4, 8, 256)
+
+    for p in range(3):
+        multiply(p, 0)
+    for p in range(3):
+        forward_unit(p, 2)
+    for d in (3, 1, 2):
+        for p in range(3):
+            multiply(p, d)
+    for pair in one.values():
+        for copy in pair:
+            copy.wait_send()
+    for pair in two.values():
+        for copy in pair:
+            copy.wait_send()
+
     lanes = lax.broadcasted_iota(jnp.int32, (512, 128), 1)
-    table = rows[:, 7168:7296].astype(F32)
+    table = rows[:, :, :, :, 7168:7296].astype(F32).reshape(512, 128)
     hidden = []
     for e in range(2):
         expert = dp * 2 + e
         mine = (lanes == expert) | (lanes == expert + 32)
         weight = jnp.sum(jnp.where(mine, table, 0.0), axis=1, keepdims=True)
-        gate_act = acc[:, e * 512:e * 512 + 256]
-        up_act = acc[:, e * 512 + 256:e * 512 + 512]
+        gate_act = acc[:, :, :, :, e * 512:e * 512 + 256].reshape(512, 256)
+        up_act = acc[:, :, :, :, e * 512 + 256:e * 512 + 512].reshape(512, 256)
         hidden.append((gate_act / (1.0 + jnp.exp(-gate_act)) * up_act * weight).astype(BF16))
     hidden = jnp.concatenate(hidden, axis=1)
 
-    def produce(p):
+    half_in = ((h0l, h0r), (h1l, h1r), (h2l, h2r))
+    full_in = ((f0l, f0r), (f1l, f1r), (f2l, f2r))
+    sums0, sums1, sums2 = (s0_send, s0_recv), (s1_send, s1_recv), (s2_send, s2_recv)
+    sums = (sums0, sums1, sums2)
+    far, near, base = {}, {}, {}
+
+    def spot(level, p, d, offset):
+        a, b, c = order[p]
+        if level == 0:
+            return (None, shifted(b, d), shifted(c, offset)), c
+        if level == 1:
+            return (None, shifted(b, offset), at[c]), b
+        return (shifted(a, offset), at[b], at[c]), a
+
+    def landing(refs, level, p, d, k, width):
+        lead = (p, d) if level == 0 else (p,)
+        return refs[level][k].at[lead + (every,) * (1 if level == 2 else 2) + (pl.ds(0, width),)]
+
+    def send_far(level, p, d):
+        slot = ((p * 4 + d) if level == 0 else p) * 4
+        far[level, p, d] = []
+        for k, sign in enumerate(signs):
+            values, axis = spot(level, p, d, 2)
+            start, width = halves(*OUT_PARTS[p])[k]
+            far[level, p, d].append(
+                push(
+                    obuf.at[block(p, values, start, width)],
+                    landing(half_in, level, p, d, k, width), *sums[level], slot + k, axis, sign,
+                )
+            )
+
+    def send_near(level, p, d, k):
+        slot = ((p * 4 + d) if level == 0 else p) * 4
+        far[level, p, d][k].wait_recv()
+        values, axis = spot(level, p, d, signs[k])
+        start, width = halves(*OUT_PARTS[p])[k]
+        half = block(p, values, start, width)
+        obuf[half] = (
+            obuf[half].astype(F32) + landing(half_in, level, p, d, k, width)[...].astype(F32)
+        ).astype(BF16)
+        near[level, p, d, k] = push(
+            obuf.at[block(p, values, *OUT_PARTS[p])],
+            landing(full_in, level, p, d, k, OUT_PARTS[p][1]), *sums[level], slot + 2 + k, axis,
+            signs[k],
+        )
+
+    def own_sum(level, p, d):
+        values, _ = spot(level, p, d, 0)
+        where = block(p, values, *OUT_PARTS[p])
+        total = obuf[where].astype(F32)
+        for k in range(2):
+            near[level, p, d, k].wait_recv()
+            total = total + landing(full_in, level, p, d, k, OUT_PARTS[p][1])[...].astype(F32)
+        if level < 2:
+            obuf[where] = total.astype(BF16)
+        return total
+
+    for p in range(3):
         start, width = OUT_PARTS[p]
         done = 0
         while done < width:
@@ -473,16 +576,38 @@
                 dot(hidden, down_w[:, cols]).reshape(4, 4, 4, 8, size).astype(BF16)
             )
             done += size
-
-    def finish(p, cols, total):
+        for d in (2, 1, 3, 0):
+            send_far(0, p, d)
+    for d in (2, 1, 3, 0):
+        for p in range(3):
+            for k in range(2):
+                send_near(0, p, d, k)
+    for p in range(3):
+        own_sum(0, p, 2)
+        send_far(1, p, 0)
+    for k, d in enumerate((1, 3)):
+        for p in range(3):
+            own_sum(0, p, d)
+            send_near(1, p, 0, k)
+    for p in range(3):
+        own_sum(0, p, 0)
+    for p in range(3):
+        own_sum(1, p, 0)
+        send_far(2, p, 0)
+    for k in range(2):
+        for p in range(3):
+            send_near(2, p, 0, k)
+    for p in range(3):
+        total = own_sum(2, p, 0)
+        cols = pl.ds(*OUT_PARTS[p])
         total = total + stream[:, cols].astype(F32)
         out[0, :, cols] = total[0:4].astype(BF16)
         out[1, :, cols] = total[4:8].astype(BF16)
-
-    ring_sum(
-        at, [o[::-1] for o in order], OUT_PARTS, obuf, ((h0l, h0r), (h1l, h1r), (h2l, h2r)),
-        ((f0l, f0r), (f1l, f1r), (f2l, f2r)), rs_send, rs_recv, neighbour, produce, finish,
-    )
+    for pair in far.values():
+        for copy in pair:
+            copy.wait_send()
+    for copy in near.values():
+        copy.wait_send()
 
 
 def per_device(
@@ -542,16 +667,15 @@
 
     scratch = [
         pltpu.VMEM((4, 4, 4, 8, ROW), BF16),
-        pltpu.VMEM((512, ROW), BF16),
         pltpu.VMEM((model, 1024), BF16),
         pltpu.VMEM((512, model), BF16),
-        pltpu.VMEM((512, 1024), F32),
+        pltpu.VMEM((4, 4, 4, 8, 1024), F32),
         pltpu.VMEM((4, 4, 4, 8, model), BF16),
     ]
     for shape in ((4, 4), (4,), ()):
         scratch += rings(3, shape, 1280)
         scratch += rings(3, shape, 2432)
-    scratch += [dma((36,)), dma((36,)), dma((36,)), dma((36,)), dma((6,)), dma((6,)), dma((6,))]
+    scratch += [dma((n,)) for n in (12, 12, 12, 12, 48, 48, 48, 48, 12, 12, 12, 12, 6, 6, 6)]
     result = pl.pallas_call(
         expert_kernel,
         out_shape=jax.ShapeDtypeStruct(residual.shape, BF16),

time: 199 us -> 188 us (0.945)
  Pallas kernels: 194 us -> 184 us
    pallas_call x1, Pallas kernels: 94.3 us -> 83.4 us  [per_device(): pl.pallas_call(expert_kernel, out_shape=jax.ShapeDtypeStruct(residual.sha...]
where the time goes in v3:
time: 188 us
  Pallas kernels  184 us (98%)
  local copies, waits for them, and re-layouts  3.02 us (2%)
    pallas_call x1, Pallas kernels, per_device(): pl.pallas_call(attention_kernel, out_shape=(jax.ShapeDtypeStruct((8, mode...  100 us
    pallas_call x1, Pallas kernels, per_device(): pl.pallas_call(expert_kernel, out_shape=jax.ShapeDtypeStruct(residual.sha...  83.4 us

profile of v3, /device:TPU:0, one launch (start us, length us, event | category | flops | bytes accessed | tf_op | source)
XLA Modules:
  0.0 188.0 jit_solution(12968511409844150720)
XLA Ops:
  0.0 0.1 pad.2.clone
  0.1 0.8 select_reduce_fusion
  0.9 0.7 maximum_maximum_fusion.mix
  1.6 1.4 copy.17.plan
  2.9 100.2 %attention.1 = (bf16[8,7168]{1,0:T(8,128)(2,1)}, bf16[8,7168]{1,0:T(8,128)(2,1)}) custom-call(s32[1,16,2]{2,1,0:T(8,128)} %copy.17.plan, s32[4,8]{1,0:T(4,128)} %tab.1, s32[4]{0:T(128)} %lens.1, bf16[24,576,128]{2,1,0:T(8,128)(2,1)} %pool.1, bf16[2,4,64,576]{3,2,1,0:T(8,128)(2,1)} %queries.1, bf16[2,4,576]{2,1,0:T(4,128)(2,1)} %new_latent.1, ...), custom_call_target="tpu_custom_call" | custom-call | tf_op jit(solution)/shard_map/attention/pallas_call | solution.py:645
  103.1 83.4 %experts.1 = bf16[2,4,7168]{2,1,0:T(4,128)(2,1)} custom-call(bf16[8,7168]{1,0:T(8,128)(2,1)} %get-tuple-element.7.normed, bf16[8,128]{1,0:T(8,128)(2,1)} %maximum_maximum_fusion.mix, bf16[8,7168]{1,0:T(8,128)(2,1)} %get-tuple-element.8.stream, bf16[2,7168,128]{2,1,0:T(8,128)(2,1)} %gate.1, bf16[2,7168,128]{2,1,0:T(8,128)(2,1)} %up.1, bf16[2,128,7168]{2,1,0:T(8,128)(2,1)} %down.1), custom_call_target="tpu_custom_call" | custom-call | tf_op jit(solution)/shard_map/experts/pallas_call | solution.py:679
  186.5 1.6 copy.19
  (2 shorter events, 0.0 us)

commit v4 on v2

--- a/solution.py
+++ b/solution.py
@@ -30,16 +30,21 @@
     return (start, first), (start + first, width - first)
 
 
-def ring_sum(at, orders, parts, buf, half_in, full_in, sends, recvs, neighbour, produce, finish):
+def ring_sum(
+    at, orders, streams, parts, buf, half_in, full_in, sends, recvs, neighbour, produce, finish
+):
     axes = len(orders[0])
     count = len(parts)
-
-    def place(reduced, axis, value):
+    signs = (1, -1)
+    far, near = {}, {}
+
+    def place(phase, p, offset):
         where = [slice(None)] * axes
-        for a in reduced:
+        for a in orders[p][:phase]:
             where[a] = at[a]
-        where[axis] = value
-        return tuple(where)
+        axis = orders[p][phase]
+        where[axis] = (at[axis] + offset + 4) % 4
+        return tuple(where) + (slice(None),)
 
     def landing(refs, phase, p, k, width):
         return refs[phase][k].at[(p,) + (slice(None),) * (axes - phase) + (pl.ds(0, width),)]
@@ -56,62 +61,59 @@
         copy.start()
         return copy
 
+    def send_far(phase, p):
+        for k in range(2):
+            start, width = halves(*parts[p])[k]
+            far[phase, p, k] = push(
+                buf.at[place(phase, p, 2) + (pl.ds(start, width),)],
+                landing(half_in, phase, p, k, width),
+                (phase * count + p) * 4 + k, orders[p][phase], signs[k],
+            )
+
+    def send_near(phase, p, k):
+        far[phase, p, k].wait_recv()
+        start, width = halves(*parts[p])[k]
+        half = place(phase, p, signs[k]) + (pl.ds(start, width),)
+        buf[half] = (
+            buf[half].astype(F32) + landing(half_in, phase, p, k, width)[...].astype(F32)
+        ).astype(BF16)
+        near[phase, p, k] = push(
+            buf.at[place(phase, p, signs[k]) + (pl.ds(*parts[p]),)],
+            landing(full_in, phase, p, k, parts[p][1]),
+            (phase * count + p) * 4 + 2 + k, orders[p][phase], signs[k],
+        )
+
+    def own_sum(phase, p):
+        where = place(phase, p, 0) + (pl.ds(*parts[p]),)
+        total = buf[where].astype(F32)
+        for k in range(2):
+            near[phase, p, k].wait_recv()
+            total = total + landing(full_in, phase, p, k, parts[p][1])[...].astype(F32)
+        if phase < axes - 1:
+            buf[where] = total.astype(BF16)
+        return total
+
     for phase in range(axes):
-        ones = []
-        for p in range(count):
-            if phase == 0:
-                produce(p)
-            axis, reduced = orders[p][phase], orders[p][:phase]
-            pair = []
-            for k, sign in enumerate((1, -1)):
-                start, width = halves(*parts[p])[k]
-                far = place(reduced, axis, (at[axis] + 2) % 4) + (slice(None), pl.ds(start, width))
-                pair.append(
-                    push(
-                        buf.at[far], landing(half_in, phase, p, k, width),
-                        (phase * count + p) * 4 + k, axis, sign,
-                    )
-                )
-            ones.append(pair)
-        twos = []
-        for p in range(count):
-            axis, reduced = orders[p][phase], orders[p][:phase]
-            pair = []
-            for k, sign in enumerate((1, -1)):
-                ones[p][k].wait_recv()
-                start, width = halves(*parts[p])[k]
-                near = place(reduced, axis, (at[axis] + sign + 4) % 4)
-                half = near + (slice(None), pl.ds(start, width))
-                buf[half] = (
-                    buf[half].astype(F32) + landing(half_in, phase, p, k, width)[...].astype(F32)
-                ).astype(BF16)
-                whole = near + (slice(None), pl.ds(*parts[p]))
-                pair.append(
-                    push(
-                        buf.at[whole], landing(full_in, phase, p, k, parts[p][1]),
-                        (phase * count + p) * 4 + 2 + k, axis, sign,
-                    )
-                )
-            twos.append(pair)
-        for p in range(count):
-            axis, reduced = orders[p][phase], orders[p][:phase]
-            for k in range(2):
-                ones[p][k].wait_send()
-                twos[p][k].wait()
-            start, width = parts[p]
-            own = place(reduced, axis, at[axis]) + (slice(None), pl.ds(start, width))
-            total = (
-                buf[own].astype(F32)
-                + landing(full_in, phase, p, 0, width)[...].astype(F32)
-                + landing(full_in, phase, p, 1, width)[...].astype(F32)
-            )
-            if phase < axes - 1:
-                buf[own] = total.astype(BF16)
-            else:
-                finish(p, pl.ds(start, width), total)
-
-
-PROJ_PARTS = ((0, 3584), (3584, 3584))
+        for stream in streams:
+            for p in stream:
+                if phase == 0:
+                    produce(p)
+                else:
+                    own_sum(phase - 1, p)
+                send_far(phase, p)
+        for stream in streams:
+            for p in stream:
+                for k in range(2):
+                    send_near(phase, p, k)
+    for stream in streams:
+        for p in stream:
+            finish(p, pl.ds(*parts[p]), own_sum(axes - 1, p))
+    for copy in list(far.values()) + list(near.values()):
+        copy.wait_send()
+
+
+PROJ_PARTS = ((0, 1792), (3584, 1792), (1792, 1792), (5376, 1792))
+PROJ_ORDERS = ((1, 0), (0, 1), (1, 0), (0, 1))
 
 
 def attention_kernel(
@@ -143,7 +145,7 @@
 
     for c in range(2):
         def pick(i, carry):
-            outgoing[c, i // 4, i % 4] = pool[jnp.maximum(plan[0, i, c], 0)]
+            outgoing[c, i // 4, i % 4] = pool[jnp.maximum(plan[0, c, i], 0)]
             return carry
 
         lax.fori_loop(0, groups, pick, 0)
@@ -289,7 +291,7 @@
         wide_sum[:, cols] = total
 
     ring_sum(
-        at, ((1, 0), (0, 1)), PROJ_PARTS, part, ((h0l, h0r), (h1l, h1r)),
+        at, PROJ_ORDERS, ((0, 1), (2, 3)), PROJ_PARTS, part, ((h0l, h0r), (h1l, h1r)),
         ((f0l, f0r), (f1l, f1r)), part_s, part_r, neighbour, produce, finish,
     )
 
@@ -311,22 +313,25 @@
         normed_out[:, cols] = (wide * scale * gain[:, cols]).astype(BF16)
 
 
-PARTS = ((0, 2432), (2432, 2432), (4864, 2432))
-OUT_PARTS = ((0, 2432), (2432, 2432), (4864, 2304))
+PARTS = ((0, 1280), (2432, 1280), (4864, 1280), (1280, 1152), (3712, 1152), (6144, 1152))
+OUT_PARTS = PARTS[:5] + ((6144, 1024),)
+STREAMS = ((0, 1, 2), (3, 4, 5))
 ROW = 7296
 
 
 def expert_kernel(
     normed, mix, stream, gate, up, down,
     out,
-    rows_buf, rows, hid_w, down_w, acc, obuf,
+    rows, hid_w, down_w, acc, obuf,
     h0l, h0r, f0l, f0r, h1l, h1r, f1l, f1r, h2l, h2r, f2l, f2r,
-    ag_send, ag_recv, rs_send, rs_recv, w_send, w_recv, w_local,
+    g_send, g_recv, s_send, s_recv, w_send, w_recv, w_local,
 ):
     dp = lax.axis_index("dp")
     tp = lax.axis_index("tp")
     at = (dp // 4, dp % 4, tp // 2)
     core = tp % 2
+    signs = (1, -1)
+    every = slice(None)
 
     def neighbour(axis, sign):
         new = list(at)
@@ -337,28 +342,22 @@
 
     barrier = pltpu.get_barrier_semaphore()
     for axis in range(3):
-        for sign in (1, -1):
+        for sign in signs:
             pl.semaphore_signal(
                 barrier, inc=1, device_id=neighbour(axis, sign), device_id_type=MESH
             )
     pl.semaphore_signal(barrier, inc=1, device_id=partner, device_id_type=MESH)
 
-    rows_buf[at[0], at[1], at[2], :, 0:7168] = normed[...]
-    rows_buf[at[0], at[1], at[2], :, 7168:7296] = mix[...]
+    rows[at[0], at[1], at[2], :, 0:7168] = normed[...]
+    rows[at[0], at[1], at[2], :, 7168:7296] = mix[...]
     local = []
     remote = []
 
     def spots(e, which):
         if which < 2:
             base = e * 512 + which * 256
-            return (
-                hid_w.at[:, pl.ds(base, 128)],
-                hid_w.at[:, pl.ds(base + 128, 128)],
-            )
-        return (
-            down_w.at[pl.ds(e * 256, 128)],
-            down_w.at[pl.ds(e * 256 + 128, 128)],
-        )
+            return hid_w.at[:, pl.ds(base, 128)], hid_w.at[:, pl.ds(base + 128, 128)]
+        return down_w.at[pl.ds(e * 256, 128)], down_w.at[pl.ds(e * 256 + 128, 128)]
 
     for e in range(2):
         for which, ref in enumerate((gate, up, down)):
@@ -379,100 +378,112 @@
         copy.start()
     pl.semaphore_wait(barrier, 7)
 
-    order = [(p, (p + 1) % 3, (p + 2) % 3) for p in range(3)]
-
-    def place(known, axis, value):
-        where = [at[0], at[1], at[2]]
-        for a in known:
-            where[a] = slice(None)
-        where[axis] = value
-        return tuple(where)
-
-    def push(ref, dst, sends, recvs, slot, axis, sign):
-        return pltpu.make_async_remote_copy(
+    order = [(p % 3, (p + 1) % 3, (p + 2) % 3) for p in range(6)]
+
+    def shifted(axis, offset):
+        return (at[axis] + offset + 4) % 4
+
+    def block(p, values, start, width):
+        where = [None] * 3
+        for axis, value in zip(order[p], values):
+            where[axis] = every if value is None else value
+        return tuple(where) + (every, pl.ds(start, width))
+
+    def known(phase, p, offset):
+        values = [None] * phase + [shifted(order[p][phase], offset)]
+        return values + [at[axis] for axis in order[p][phase + 1:]]
+
+    def push(phase, p, offset, k, step, columns):
+        ref = rows.at[block(p, known(phase, p, offset), *columns)]
+        slot = (phase * 6 + p) * 4 + step * 2 + k
+        copy = pltpu.make_async_remote_copy(
             src_ref=ref,
-            dst_ref=dst,
-            send_sem=sends.at[slot],
-            recv_sem=recvs.at[slot],
-            device_id=neighbour(axis, sign),
+            dst_ref=ref,
+            send_sem=g_send.at[slot],
+            recv_sem=g_recv.at[slot],
+            device_id=neighbour(order[p][phase], signs[k]),
             device_id_type=MESH,
         )
+        copy.start()
+        return copy
+
+    one, two = {}, {}
+
+    def step_one(phase, p):
+        if phase > 0:
+            for k in range(2):
+                two[phase - 1, p, k].wait_recv()
+        for k in range(2):
+            one[phase, p, k] = push(phase, p, 0, k, 0, PARTS[p])
+
+    def step_two(phase, p):
+        for k in range(2):
+            one[phase, p, k].wait_recv()
+            two[phase, p, k] = push(phase, p, -signs[k], k, 1, halves(*PARTS[p])[k])
 
     for phase in range(3):
-        ones = []
-        for p in range(3):
-            axis = order[p][phase]
-            known = order[p][:phase]
-            start, width = PARTS[p]
-            own = place(known, axis, at[axis]) + (slice(None), pl.ds(start, width))
-            slot = (phase * 3 + p) * 4
-            pair = [
-                push(rows_buf.at[own], rows_buf.at[own], ag_send, ag_recv, slot + k, axis, sign)
-                for k, sign in enumerate((1, -1))
-            ]
-            for copy in pair:
-                copy.start()
-            ones.append(pair)
+        for group in STREAMS:
+            for p in group:
+                step_one(phase, p)
         if phase == 0:
             for copy in remote:
                 copy.start()
-        twos = []
-        for p in range(3):
-            axis = order[p][phase]
-            known = order[p][:phase]
-            slot = (phase * 3 + p) * 4 + 2
-            pair = []
-            for k, sign in enumerate((1, -1)):
-                ones[p][k].wait_recv()
-                start, width = halves(*PARTS[p])[k]
-                came = place(known, axis, (at[axis] - sign + 4) % 4) + (
-                    slice(None), pl.ds(start, width),
-                )
-                copy = push(
-                    rows_buf.at[came], rows_buf.at[came], ag_send, ag_recv, slot + k, axis, sign
-                )
-                copy.start()
-                pair.append(copy)
-            twos.append(pair)
-        for p in range(3):
-            for k in range(2):
-                ones[p][k].wait_send()
-                twos[p][k].wait()
+            acc[...] = jnp.zeros_like(acc)
+        if phase < 2:
+            for group in STREAMS:
+                for p in group:
+                    step_two(phase, p)
 
     for copy in local:
         copy.wait()
     for copy in remote:
         copy.wait()
 
-    for y in range(4):
-        rows[pl.ds(y * 128, 128), :] = (
-            rows_buf[y].astype(F32).reshape(128, ROW).astype(BF16)
-        )
-    for n in range(4):
-        cols = pl.ds(n * 256, 256)
-        acc[:, cols] = dot(rows[:, 0:7168], hid_w[:, cols])
+    def multiply(p, offset):
+        start, width = OUT_PARTS[p]
+        lhs = rows[block(p, known(2, p, offset), start, width)]
+        lhs = lhs.astype(F32).reshape(128, width).astype(BF16)
+        for n in range(4):
+            cols = (n * 256, 256)
+            where = block(p, known(2, p, offset), *cols)
+            product = dot(lhs, hid_w[pl.ds(start, width), pl.ds(*cols)])
+            acc[where] = acc[where] + product.reshape(4, 4, 8, 256)
+
+    for p in range(6):
+        multiply(p, 0)
+    for group in STREAMS:
+        for p in group:
+            step_two(2, p)
+    for p in range(6):
+        multiply(p, 1)
+        multiply(p, -1)
+    for p in range(6):
+        for k in range(2):
+            two[2, p, k].wait_recv()
+        multiply(p, 2)
+    for copy in list(one.values()) + list(two.values()):
+        copy.wait_send()
+
     lanes = lax.broadcasted_iota(jnp.int32, (512, 128), 1)
-    table = rows[:, 7168:7296].astype(F32)
+    table = rows[:, :, :, :, 7168:7296].astype(F32).reshape(512, 128)
     hidden = []
     for e in range(2):
         expert = dp * 2 + e
         mine = (lanes == expert) | (lanes == expert + 32)
         weight = jnp.sum(jnp.where(mine, table, 0.0), axis=1, keepdims=True)
-        gate_act = acc[:, e * 512:e * 512 + 256]
-        up_act = acc[:, e * 512 + 256:e * 512 + 512]
+        gate_act = acc[:, :, :, :, e * 512:e * 512 + 256].reshape(512, 256)
+        up_act = acc[:, :, :, :, e * 512 + 256:e * 512 + 512].reshape(512, 256)
         hidden.append((gate_act / (1.0 + jnp.exp(-gate_act)) * up_act * weight).astype(BF16))
     hidden = jnp.concatenate(hidden, axis=1)
 
     def produce(p):
         start, width = OUT_PARTS[p]
-        done = 0
-        while done < width:
+        for done in range(0, width, 256):
             size = min(256, width - done)
             cols = pl.ds(start + done, size)
             obuf[:, :, :, :, cols] = (
                 dot(hidden, down_w[:, cols]).reshape(4, 4, 4, 8, size).astype(BF16)
             )
-            done += size
 
     def finish(p, cols, total):
         total = total + stream[:, cols].astype(F32)
@@ -480,8 +491,8 @@
         out[1, :, cols] = total[4:8].astype(BF16)
 
     ring_sum(
-        at, [o[::-1] for o in order], OUT_PARTS, obuf, ((h0l, h0r), (h1l, h1r), (h2l, h2r)),
-        ((f0l, f0r), (f1l, f1r), (f2l, f2r)), rs_send, rs_recv, neighbour, produce, finish,
+        at, [o[::-1] for o in order], STREAMS, OUT_PARTS, obuf, ((h0l, h0r), (h1l, h1r), (h2l, h2r)),
+        ((f0l, f0r), (f1l, f1r), (f2l, f2r)), s_send, s_recv, neighbour, produce, finish,
     )
 
 
@@ -514,9 +525,9 @@
         pltpu.VMEM((8, model), F32),
     ]
     for shape in ((4,), ()):
-        scratch += rings(2, shape, 1792)
-        scratch += rings(2, shape, 3584)
-    scratch += [dma((24,)), dma((24,)), dma((15,)), dma((15,)), dma((16,)), dma((16,)), dma((5,))]
+        scratch += rings(4, shape, 896)
+        scratch += rings(4, shape, 1792)
+    scratch += [dma((24,)), dma((24,)), dma((15,)), dma((15,)), dma((32,)), dma((32,)), dma((5,))]
     stream, normed = pl.pallas_call(
         attention_kernel,
         out_shape=(
@@ -531,7 +542,7 @@
         ),
         name="attention",
     )(
-        send_plan, tables, lengths, cache_pool, queries, new_latent, value_up,
+        jnp.transpose(send_plan, (0, 2, 1)), tables, lengths, cache_pool, queries, new_latent, value_up,
         out_proj, residual, norm_gain.reshape(1, model),
     )
 
@@ -542,16 +553,15 @@
 
     scratch = [
         pltpu.VMEM((4, 4, 4, 8, ROW), BF16),
-        pltpu.VMEM((512, ROW), BF16),
         pltpu.VMEM((model, 1024), BF16),
         pltpu.VMEM((512, model), BF16),
-        pltpu.VMEM((512, 1024), F32),
+        pltpu.VMEM((4, 4, 4, 8, 1024), F32),
         pltpu.VMEM((4, 4, 4, 8, model), BF16),
     ]
     for shape in ((4, 4), (4,), ()):
-        scratch += rings(3, shape, 1280)
-        scratch += rings(3, shape, 2432)
-    scratch += [dma((36,)), dma((36,)), dma((36,)), dma((36,)), dma((6,)), dma((6,)), dma((6,))]
+        scratch += rings(6, shape, 640)
+        scratch += rings(6, shape, 1280)
+    scratch += [dma((n,)) for n in (72, 72, 72, 72, 6, 6, 6)]
     result = pl.pallas_call(
         expert_kernel,
         out_shape=jax.ShapeDtypeStruct(residual.shape, BF16),

time: 199 us -> 183 us (0.920)
  Pallas kernels: 194 us -> 179 us
    pallas_call x1, Pallas kernels: 94.3 us -> 81.6 us  [per_device(): pl.pallas_call(expert_kernel, out_shape=jax.ShapeDtypeStruct(residual.sha...]
    pallas_call x1, Pallas kernels: 100 us -> 97.7 us  [per_device(): pl.pallas_call(attention_kernel, out_shape=(jax.ShapeDtypeStruct((8, mode...]
where the time goes in v4:
time: 183 us; the launch traced here: 182 us
  Pallas kernels  179 us (98%)
    pallas_call x1, Pallas kernels, per_device(): pl.pallas_call(attention_kernel, out_shape=(jax.ShapeDtypeStruct((8, mode...  97.7 us
    pallas_call x1, Pallas kernels, per_device(): pl.pallas_call(expert_kernel, out_shape=jax.ShapeDtypeStruct(residual.sha...  81.6 us

profile of v4, /device:TPU:0, one launch (start us, length us, event | category | flops | bytes accessed | tf_op | source)
XLA Modules:
  0.0 182.4 jit_solution(2196869817538312179)
XLA Ops:
  0.0 0.1 pad.2.clone
  0.1 0.8 select_reduce_fusion
  0.9 0.7 maximum_maximum_fusion.mix
  1.5 97.7 %attention.1 = (bf16[8,7168]{1,0:T(8,128)(2,1)}, bf16[8,7168]{1,0:T(8,128)(2,1)}) custom-call(s32[1,2,16]{2,1,0:T(2,128)} %bitcast.7, s32[4,8]{1,0:T(4,128)} %tab.1, s32[4]{0:T(128)} %lens.1, bf16[24,576,128]{2,1,0:T(8,128)(2,1)} %pool.1, bf16[2,4,64,576]{3,2,1,0:T(8,128)(2,1)} %queries.1, bf16[2,4,576]{2,1,0:T(4,128)(2,1)} %new_latent.1, ...), custom_call_target="tpu_custom_call" | custom-call | tf_op jit(solution)/shard_map/attention/pallas_call | solution.py:531
  99.3 81.6 %experts.1 = bf16[2,4,7168]{2,1,0:T(4,128)(2,1)} custom-call(bf16[8,7168]{1,0:T(8,128)(2,1)} %get-tuple-element.7.normed, bf16[8,128]{1,0:T(8,128)(2,1)} %maximum_maximum_fusion.mix, bf16[8,7168]{1,0:T(8,128)(2,1)} %get-tuple-element.8.stream, bf16[2,7168,128]{2,1,0:T(8,128)(2,1)} %gate.1, bf16[2,7168,128]{2,1,0:T(8,128)(2,1)} %up.1, bf16[2,128,7168]{2,1,0:T(8,128)(2,1)} %down.1), custom_call_target="tpu_custom_call" | custom-call | tf_op jit(solution)/shard_map/experts/pallas_call | solution.py:565
  180.8 1.6 copy.17
  (2 shorter events, 0.0 us)

commit v5 on v4

--- a/solution.py
+++ b/solution.py
@@ -31,7 +31,7 @@
 
 
 def ring_sum(
-    at, orders, streams, parts, buf, half_in, full_in, sends, recvs, neighbour, produce, finish
+    at, orders, streams, parts, buf, half_in, full_in, last_in, sends, recvs, neighbour, produce, finish
 ):
     axes = len(orders[0])
     count = len(parts)
@@ -83,17 +83,32 @@
             (phase * count + p) * 4 + 2 + k, orders[p][phase], signs[k],
         )
 
+    def send_last(p):
+        phase = axes - 1
+        for offset in (2, 1, 3):
+            far[phase, p, offset] = push(
+                buf.at[place(phase, p, offset) + (pl.ds(*parts[p]),)],
+                last_in.at[p, offset - 1, :, pl.ds(0, parts[p][1])],
+                (phase * count + p) * 4 + offset - 1, orders[p][phase], offset,
+            )
+
+    def last_sum(p):
+        phase = axes - 1
+        total = buf[place(phase, p, 0) + (pl.ds(*parts[p]),)].astype(F32)
+        for offset in (1, 3, 2):
+            far[phase, p, offset].wait_recv()
+            total = total + last_in[p, offset - 1, :, pl.ds(0, parts[p][1])].astype(F32)
+        return total
+
     def own_sum(phase, p):
         where = place(phase, p, 0) + (pl.ds(*parts[p]),)
         total = buf[where].astype(F32)
         for k in range(2):
             near[phase, p, k].wait_recv()
             total = total + landing(full_in, phase, p, k, parts[p][1])[...].astype(F32)
-        if phase < axes - 1:
-            buf[where] = total.astype(BF16)
-        return total
-
-    for phase in range(axes):
+        buf[where] = total.astype(BF16)
+
+    for phase in range(axes - 1):
         for stream in streams:
             for p in stream:
                 if phase == 0:
@@ -107,7 +122,11 @@
                     send_near(phase, p, k)
     for stream in streams:
         for p in stream:
-            finish(p, pl.ds(*parts[p]), own_sum(axes - 1, p))
+            own_sum(axes - 2, p)
+            send_last(p)
+    for stream in streams:
+        for p in stream:
+            finish(p, pl.ds(*parts[p]), last_sum(p))
     for copy in list(far.values()) + list(near.values()):
         copy.wait_send()
 
@@ -117,10 +136,10 @@
 
 
 def attention_kernel(
-    plan, tab, lens, pool, queries, new_latent, value_up, proj_hbm, resid, gain,
-    stream_out, normed_out,
+    plan, tab, lens, pool, queries, new_latent, value_up, proj_hbm, resid, gain, routes, route_weight,
+    stream_out, normed_out, mix_out,
     outgoing, middle, near_fwd, far_fwd, arrived, keys, fresh, lat_send, lat_recv, proj, part,
-    wide_sum, h0l, h0r, f0l, f0r, h1l, h1r, f1l, f1r,
+    wide_sum, h0l, h0r, f0l, f0r, last,
     mig_s, mig_r, lat_s, lat_r, part_s, part_r, local_sem,
 ):
     groups = 16
@@ -151,6 +170,16 @@
         lax.fori_loop(0, groups, pick, 0)
     for k in range(2):
         fresh[k] = new_latent[k].astype(F32)
+
+    named = jnp.concatenate([routes[0], routes[1]], axis=0)
+    given = jnp.concatenate([route_weight[0], route_weight[1]], axis=0)
+    lanes = lax.broadcasted_iota(jnp.int32, (8, 128), 1)
+    dense = jnp.zeros((8, 128), F32)
+    for k in range(8):
+        hit = ((lanes & 31) == named[:, k:k + 1]) & (lanes < 64)
+        dense = dense + jnp.where(hit, given[:, k:k + 1], 0.0)
+    high = dense.astype(BF16).astype(F32)
+    mix_out[...] = jnp.where(lanes < 32, high, dense - high).astype(BF16)
     pl.semaphore_wait(barrier, groups - 1)
 
     def push(src, dst, slot, axis, sign):
@@ -207,17 +236,6 @@
         for copy in second + kept:
             copy.wait()
 
-    def exchange(src, dst, send_sem, recv_sem, shift):
-        peer = lax.rem(me + shift, groups)
-        return pltpu.make_async_remote_copy(
-            src_ref=src(peer),
-            dst_ref=dst(me),
-            send_sem=send_sem.at[shift - 1],
-            recv_sem=recv_sem.at[shift - 1],
-            device_id=(peer, lane),
-            device_id_type=MESH,
-        )
-
     row = lax.broadcasted_iota(jnp.int32, (128, 128), 0)
     col = lax.broadcasted_iota(jnp.int32, (128, 128), 1)
     reorder = jnp.where(
@@ -256,14 +274,23 @@
         lat_send[:, pl.ds(s, 1)] = latent.reshape(16, 1, 8, LAT).astype(BF16)
         return carry
 
-    lax.fori_loop(0, 4, attend, 0)
-
-    moves = [
-        exchange(lambda p: lat_send.at[p], lambda m: lat_recv.at[m], lat_s, lat_r, shift)
-        for shift in range(1, groups)
-    ]
-    for move in moves:
-        move.start()
+    moves = []
+    for half in range(2):
+        lax.fori_loop(2 * half, 2 * half + 2, attend, 0)
+        pair = pl.ds(2 * half, 2)
+        for shift in range(1, groups):
+            peer = lax.rem(me + shift, groups)
+            slot = half * (groups - 1) + shift - 1
+            move = pltpu.make_async_remote_copy(
+                src_ref=lat_send.at[peer, pair],
+                dst_ref=lat_recv.at[me, pair],
+                send_sem=lat_s.at[slot],
+                recv_sem=lat_r.at[slot],
+                device_id=(peer, lane),
+                device_id_type=MESH,
+            )
+            move.start()
+            moves.append(move)
     lat_recv[me] = lat_send[me]
     for move in moves:
         move.wait()
@@ -291,8 +318,8 @@
         wide_sum[:, cols] = total
 
     ring_sum(
-        at, PROJ_ORDERS, ((0, 1), (2, 3)), PROJ_PARTS, part, ((h0l, h0r), (h1l, h1r)),
-        ((f0l, f0r), (f1l, f1r)), part_s, part_r, neighbour, produce, finish,
+        at, PROJ_ORDERS, ((0, 1), (2, 3)), PROJ_PARTS, part, ((h0l, h0r),),
+        ((f0l, f0r),), last, part_s, part_r, neighbour, produce, finish,
     )
 
     chunk = 1024
@@ -323,7 +350,7 @@
     normed, mix, stream, gate, up, down,
     out,
     rows, hid_w, down_w, acc, obuf,
-    h0l, h0r, f0l, f0r, h1l, h1r, f1l, f1r, h2l, h2r, f2l, f2r,
+    h0l, h0r, f0l, f0r, h1l, h1r, f1l, f1r, last,
     g_send, g_recv, s_send, s_recv, w_send, w_recv, w_local,
 ):
     dp = lax.axis_index("dp")
@@ -342,7 +369,7 @@
 
     barrier = pltpu.get_barrier_semaphore()
     for axis in range(3):
-        for sign in signs:
+        for sign in (1, 2, 3):
             pl.semaphore_signal(
                 barrier, inc=1, device_id=neighbour(axis, sign), device_id_type=MESH
             )
@@ -376,7 +403,7 @@
             )
     for copy in local:
         copy.start()
-    pl.semaphore_wait(barrier, 7)
+    pl.semaphore_wait(barrier, 10)
 
     order = [(p % 3, (p + 1) % 3, (p + 2) % 3) for p in range(6)]
 
@@ -393,15 +420,15 @@
         values = [None] * phase + [shifted(order[p][phase], offset)]
         return values + [at[axis] for axis in order[p][phase + 1:]]
 
-    def push(phase, p, offset, k, step, columns):
+    def push(phase, p, offset, slot, sign, columns):
         ref = rows.at[block(p, known(phase, p, offset), *columns)]
-        slot = (phase * 6 + p) * 4 + step * 2 + k
+        slot = (phase * 6 + p) * 4 + slot
         copy = pltpu.make_async_remote_copy(
             src_ref=ref,
             dst_ref=ref,
             send_sem=g_send.at[slot],
             recv_sem=g_recv.at[slot],
-            device_id=neighbour(order[p][phase], signs[k]),
+            device_id=neighbour(order[p][phase], sign),
             device_id_type=MESH,
         )
         copy.start()
@@ -410,16 +437,19 @@
     one, two = {}, {}
 
     def step_one(phase, p):
-        if phase > 0:
-            for k in range(2):
-                two[phase - 1, p, k].wait_recv()
+        if phase == 0:
+            for sign in (2, 1, 3):
+                two[0, p, sign - 1] = push(0, p, 0, sign - 1, sign, PARTS[p])
+            return
+        for k in range(3 if phase == 1 else 2):
+            two[phase - 1, p, k].wait_recv()
         for k in range(2):
-            one[phase, p, k] = push(phase, p, 0, k, 0, PARTS[p])
+            one[phase, p, k] = push(phase, p, 0, k, signs[k], PARTS[p])
 
     def step_two(phase, p):
         for k in range(2):
             one[phase, p, k].wait_recv()
-            two[phase, p, k] = push(phase, p, -signs[k], k, 1, halves(*PARTS[p])[k])
+            two[phase, p, k] = push(phase, p, -signs[k], 2 + k, signs[k], halves(*PARTS[p])[k])
 
     for phase in range(3):
         for group in STREAMS:
@@ -429,7 +459,7 @@
             for copy in remote:
                 copy.start()
             acc[...] = jnp.zeros_like(acc)
-        if phase < 2:
+        if phase == 1:
             for group in STREAMS:
                 for p in group:
                     step_two(phase, p)
@@ -491,8 +521,8 @@
         out[1, :, cols] = total[4:8].astype(BF16)
 
     ring_sum(
-        at, [o[::-1] for o in order], STREAMS, OUT_PARTS, obuf, ((h0l, h0r), (h1l, h1r), (h2l, h2r)),
-        ((f0l, f0r), (f1l, f1r), (f2l, f2r)), s_send, s_recv, neighbour, produce, finish,
+        at, [o[::-1] for o in order], STREAMS, OUT_PARTS, obuf, ((h0l, h0r), (h1l, h1r)),
+        ((f0l, f0r), (f1l, f1r)), last, s_send, s_recv, neighbour, produce, finish,
     )
 
 
@@ -524,18 +554,19 @@
         pltpu.VMEM((4, 4, 8, model), BF16),
         pltpu.VMEM((8, model), F32),
     ]
-    for shape in ((4,), ()):
-        scratch += rings(4, shape, 896)
-        scratch += rings(4, shape, 1792)
-    scratch += [dma((24,)), dma((24,)), dma((15,)), dma((15,)), dma((32,)), dma((32,)), dma((5,))]
-    stream, normed = pl.pallas_call(
+    scratch += rings(4, (4,), 896)
+    scratch += rings(4, (4,), 1792)
+    scratch.append(pltpu.VMEM((4, 3, 8, 1792), BF16))
+    scratch += [dma((24,)), dma((24,)), dma((30,)), dma((30,)), dma((32,)), dma((32,)), dma((5,))]
+    stream, normed, mix = pl.pallas_call(
         attention_kernel,
         out_shape=(
             jax.ShapeDtypeStruct((8, model), BF16),
             jax.ShapeDtypeStruct((8, model), BF16),
+            jax.ShapeDtypeStruct((8, 128), BF16),
         ),
-        in_specs=[smem, smem, smem, vmem, vmem, vmem, vmem, hbm, vmem, vmem],
-        out_specs=(vmem, vmem),
+        in_specs=[smem, smem, smem, vmem, vmem, vmem, vmem, hbm, vmem, vmem, vmem, vmem],
+        out_specs=(vmem, vmem, vmem),
         scratch_shapes=scratch,
         compiler_params=pltpu.CompilerParams(
             collective_id=0, has_side_effects=True, vmem_limit_bytes=56 * MIB
@@ -543,13 +574,8 @@
         name="attention",
     )(
         jnp.transpose(send_plan, (0, 2, 1)), tables, lengths, cache_pool, queries, new_latent, value_up,
-        out_proj, residual, norm_gain.reshape(1, model),
+        out_proj, residual, norm_gain.reshape(1, model), routes, route_weight,
     )
-
-    matches = routes.reshape(8, 8)[:, :, None] == jnp.arange(32, dtype=jnp.int32)[None, None, :]
-    dense = jnp.sum(jnp.where(matches, route_weight.reshape(8, 8)[:, :, None], 0.0), axis=1)
-    high = lax.reduce_precision(dense, 8, 7)
-    mix = jnp.concatenate([high, dense - high, jnp.zeros((8, 64), F32)], axis=1).astype(BF16)
 
     scratch = [
         pltpu.VMEM((4, 4, 4, 8, ROW), BF16),
@@ -558,9 +584,10 @@
         pltpu.VMEM((4, 4, 4, 8, 1024), F32),
         pltpu.VMEM((4, 4, 4, 8, model), BF16),
     ]
-    for shape in ((4, 4), (4,), ()):
+    for shape in ((4, 4), (4,)):
         scratch += rings(6, shape, 640)
         scratch += rings(6, shape, 1280)
+    scratch.append(pltpu.VMEM((6, 3, 8, 1280), BF16))
     scratch += [dma((n,)) for n in (72, 72, 72, 72, 6, 6, 6)]
     result = pl.pallas_call(
         expert_kernel,

time: 183 us -> 173 us (0.945)
  Pallas kernels: 179 us -> 172 us
    pallas_call x1, Pallas kernels: 81.6 us -> 77.5 us  [per_device(): pl.pallas_call(expert_kernel, out_shape=jax.ShapeDtypeStruct(residual.sha...]
    pallas_call x1, Pallas kernels: 97.7 us -> 94.1 us  [per_device(): pl.pallas_call(attention_kernel, out_shape=(jax.ShapeDtypeStruct((8, mode...]
where the time goes in v5:
time: 173 us
  Pallas kernels  172 us (99%)
    pallas_call x1, Pallas kernels, per_device(): pl.pallas_call(attention_kernel, out_shape=(jax.ShapeDtypeStruct((8, mode...  94.1 us
    pallas_call x1, Pallas kernels, per_device(): pl.pallas_call(expert_kernel, out_shape=jax.ShapeDtypeStruct(residual.sha...  77.5 us

profile of v5, /device:TPU:0, one launch (start us, length us, event | category | flops | bytes accessed | tf_op | source)
XLA Modules:
  0.0 173.2 jit_solution(14411460804353984746)
XLA Ops:
  0.0 94.1 %attention.1 = (bf16[8,7168]{1,0:T(8,128)(2,1)}, bf16[8,7168]{1,0:T(8,128)(2,1)}, bf16[8,128]{1,0:T(8,128)(2,1)}) custom-call(s32[1,2,16]{2,1,0:T(2,128)} %bitcast.3, s32[4,8]{1,0:T(4,128)} %tab.1, s32[4]{0:T(128)} %lens.1, bf16[24,576,128]{2,1,0:T(8,128)(2,1)} %pool.1, bf16[2,4,64,576]{3,2,1,0:T(8,128)(2,1)} %queries.1, bf16[2,4,576]{2,1,0:T(4,128)(2,1)} %new_latent.1, ...), custom_call_target="tpu_custom_call" | custom-call | tf_op jit(solution)/shard_map/attention/pallas_call | solution.py:561
  94.1 77.5 %experts.1 = bf16[2,4,7168]{2,1,0:T(4,128)(2,1)} custom-call(bf16[8,7168]{1,0:T(8,128)(2,1)} %get-tuple-element.8.normed, bf16[8,128]{1,0:T(8,128)(2,1)} %get-tuple-element.9.mix, bf16[8,7168]{1,0:T(8,128)(2,1)} %get-tuple-element.10.stream, bf16[2,7168,128]{2,1,0:T(8,128)(2,1)} %gate.1, bf16[2,7168,128]{2,1,0:T(8,128)(2,1)} %up.1, bf16[2,128,7168]{2,1,0:T(8,128)(2,1)} %down.1), custom_call_target="tpu_custom_call" | custom-call | tf_op jit(solution)/shard_map/experts/pallas_call | solution.py:592
  171.6 1.6 copy.17

commit v6 on v5

--- a/solution.py
+++ b/solution.py
@@ -194,47 +194,78 @@
         copy.start()
         return copy
 
-    def pair_at(axis, value, k):
+    def pair_at(c, axis, value, k, h):
         rest = pl.ds(0, 4) if k is None else pl.ds(2 * k, 2)
-        return (rest, value) if axis == 1 else (value, rest)
+        where = (rest, value) if axis == 1 else (value, rest)
+        return (c,) + where + (pl.ds(288 * h, 288),)
 
     def local(src, dst, n):
         copy = pltpu.make_async_copy(src, dst, local_sem.at[n])
         copy.start()
         return copy
 
-    for stage in range(2):
+    started, passed, kept = {}, {}, {}
+
+    def send_bundles(stage, h):
         source, target = (outgoing, middle) if stage == 0 else (middle, arrived)
         fwd = (near_fwd, far_fwd)[stage]
-        first, kept = [], []
         for c in range(2):
             axis = 1 - c if stage == 0 else c
             far = (at[axis] + 2) % 4
             for k, sign in enumerate((1, -1)):
-                base = ((stage * 2 + c) * 2 + k) * 3
+                base = (((stage * 2 + h) * 2 + c) * 2 + k) * 3
                 halfway = push(
-                    source.at[(c,) + pair_at(axis, far, k)], fwd.at[c, k], base, axis, sign
+                    source.at[pair_at(c, axis, far, k, h)],
+                    fwd.at[c, k, :, pl.ds(288 * h, 288)], base, axis, sign,
                 )
                 beside = push(
-                    source.at[(c,) + pair_at(axis, (at[axis] + sign + 4) % 4, None)],
-                    target.at[(c,) + pair_at(axis, at[axis], None)],
+                    source.at[pair_at(c, axis, (at[axis] + sign + 4) % 4, None, h)],
+                    target.at[pair_at(c, axis, at[axis], None, h)],
                     base + 1, axis, sign,
                 )
-                first.append((c, k, sign, axis, base, halfway, beside))
-            own = (c,) + pair_at(axis, at[axis], None)
-            kept.append(local(source.at[own], target.at[own], 1 + stage * 2 + c))
-        second = []
-        for c, k, sign, axis, base, halfway, beside in first:
-            halfway.wait_recv()
-            came = (at[axis] - sign + 4) % 4
-            second.append(
-                push(fwd.at[c, k], target.at[(c,) + pair_at(axis, came, k)], base + 2, axis, sign)
+                started[stage, h, c, k] = (halfway, beside)
+            own = pair_at(c, axis, at[axis], None, h)
+            kept[stage, h, c] = local(
+                source.at[own], target.at[own], 1 + (stage * 2 + h) * 2 + c
             )
-        for c, k, sign, axis, base, halfway, beside in first:
-            halfway.wait_send()
-            beside.wait()
-        for copy in second + kept:
-            copy.wait()
+
+    def pass_on(stage, h):
+        target = (middle, arrived)[stage]
+        fwd = (near_fwd, far_fwd)[stage]
+        for c in range(2):
+            axis = 1 - c if stage == 0 else c
+            for k, sign in enumerate((1, -1)):
+                base = (((stage * 2 + h) * 2 + c) * 2 + k) * 3
+                started[stage, h, c, k][0].wait_recv()
+                came = (at[axis] - sign + 4) % 4
+                passed[stage, h, c, k] = push(
+                    fwd.at[c, k, :, pl.ds(288 * h, 288)],
+                    target.at[pair_at(c, axis, came, k, h)], base + 2, axis, sign,
+                )
+
+    def finish_stage(stage, h):
+        for c in range(2):
+            for k in range(2):
+                started[stage, h, c, k][1].wait_recv()
+                passed[stage, h, c, k].wait_recv()
+            kept[stage, h, c].wait()
+
+    for h in range(2):
+        send_bundles(0, h)
+    for h in range(2):
+        pass_on(0, h)
+    for h in range(2):
+        finish_stage(0, h)
+        send_bundles(1, h)
+    for h in range(2):
+        pass_on(1, h)
+    for h in range(2):
+        finish_stage(1, h)
+    for halfway, beside in started.values():
+        halfway.wait_send()
+        beside.wait_send()
+    for copy in passed.values():
+        copy.wait_send()
 
     row = lax.broadcasted_iota(jnp.int32, (128, 128), 0)
     col = lax.broadcasted_iota(jnp.int32, (128, 128), 1)
@@ -557,7 +588,7 @@
     scratch += rings(4, (4,), 896)
     scratch += rings(4, (4,), 1792)
     scratch.append(pltpu.VMEM((4, 3, 8, 1792), BF16))
-    scratch += [dma((24,)), dma((24,)), dma((30,)), dma((30,)), dma((32,)), dma((32,)), dma((5,))]
+    scratch += [dma((48,)), dma((48,)), dma((30,)), dma((30,)), dma((32,)), dma((32,)), dma((9,))]
     stream, normed, mix = pl.pallas_call(
         attention_kernel,
         out_shape=(

time: 173 us -> 172 us (level)
  no operation moved by 1% of the time
where the time goes in v6:
time: 172 us
  Pallas kernels  171 us (99%)
    pallas_call x1, Pallas kernels, per_device(): pl.pallas_call(attention_kernel, out_shape=(jax.ShapeDtypeStruct((8, mode...  93.3 us
    pallas_call x1, Pallas kernels, per_device(): pl.pallas_call(expert_kernel, out_shape=jax.ShapeDtypeStruct(residual.sha...  77.4 us

profile of v6, /device:TPU:0, one launch (start us, length us, event | category | flops | bytes accessed | tf_op | source)
XLA Modules:
  0.0 172.3 jit_solution(5463528661461031378)
XLA Ops:
  0.0 93.3 %attention.1 = (bf16[8,7168]{1,0:T(8,128)(2,1)}, bf16[8,7168]{1,0:T(8,128)(2,1)}, bf16[8,128]{1,0:T(8,128)(2,1)}) custom-call(s32[1,2,16]{2,1,0:T(2,128)} %bitcast.3, s32[4,8]{1,0:T(4,128)} %tab.1, s32[4]{0:T(128)} %lens.1, bf16[24,576,128]{2,1,0:T(8,128)(2,1)} %pool.1, bf16[2,4,64,576]{3,2,1,0:T(8,128)(2,1)} %queries.1, bf16[2,4,576]{2,1,0:T(4,128)(2,1)} %new_latent.1, ...), custom_call_target="tpu_custom_call" | custom-call | tf_op jit(solution)/shard_map/attention/pallas_call | solution.py:592
  93.3 77.4 %experts.1 = bf16[2,4,7168]{2,1,0:T(4,128)(2,1)} custom-call(bf16[8,7168]{1,0:T(8,128)(2,1)} %get-tuple-element.8.normed, bf16[8,128]{1,0:T(8,128)(2,1)} %get-tuple-element.9.mix, bf16[8,7168]{1,0:T(8,128)(2,1)} %get-tuple-element.10.stream, bf16[2,7168,128]{2,1,0:T(8,128)(2,1)} %gate.1, bf16[2,7168,128]{2,1,0:T(8,128)(2,1)} %up.1, bf16[2,128,7168]{2,1,0:T(8,128)(2,1)} %down.1), custom_call_target="tpu_custom_call" | custom-call | tf_op jit(solution)/shard_map/experts/pallas_call | solution.py:623
  170.7 1.6 copy.17

commit v7 on v6

--- a/solution.py
+++ b/solution.py
@@ -136,9 +136,9 @@
 
 
 def attention_kernel(
-    plan, tab, lens, pool, queries, new_latent, value_up, proj_hbm, resid, gain, routes, route_weight,
+    plan, tab, lens, pool_hbm, queries_hbm, new_latent, value_up, proj_hbm, resid, gain, routes, route_weight,
     stream_out, normed_out, mix_out,
-    outgoing, middle, near_fwd, far_fwd, arrived, keys, fresh, lat_send, lat_recv, proj, part,
+    pool, queries, outgoing, middle, near_fwd, far_fwd, arrived, keys, fresh, lat_send, lat_recv, proj, part,
     wide_sum, h0l, h0r, f0l, f0r, last,
     mig_s, mig_r, lat_s, lat_r, part_s, part_r, local_sem,
 ):
@@ -148,8 +148,8 @@
     at = (me // 4, me % 4)
     model = proj_hbm.shape[1]
 
-    proj_copy = pltpu.make_async_copy(proj_hbm, proj, local_sem.at[0])
-    proj_copy.start()
+    pool_copy = pltpu.make_async_copy(pool_hbm, pool, local_sem.at[9])
+    pool_copy.start()
 
     def neighbour(axis, sign):
         new = list(at)
@@ -162,6 +162,12 @@
             barrier, inc=1, device_id=(lax.rem(me + shift, groups), lane), device_id_type=MESH
         )
 
+    queries_copy = pltpu.make_async_copy(queries_hbm, queries, local_sem.at[10])
+    queries_copy.start()
+    proj_copy = pltpu.make_async_copy(proj_hbm, proj, local_sem.at[0])
+    proj_copy.start()
+
+    pool_copy.wait()
     for c in range(2):
         def pick(i, carry):
             outgoing[c, i // 4, i % 4] = pool[jnp.maximum(plan[0, c, i], 0)]
@@ -305,6 +311,7 @@
         lat_send[:, pl.ds(s, 1)] = latent.reshape(16, 1, 8, LAT).astype(BF16)
         return carry
 
+    queries_copy.wait()
     moves = []
     for half in range(2):
         lax.fori_loop(2 * half, 2 * half + 2, attend, 0)
@@ -572,6 +579,8 @@
         return [pltpu.VMEM((parts,) + shape + (8, width), BF16)] * 2
 
     scratch = [
+        pltpu.VMEM(cache_pool.shape, BF16),
+        pltpu.VMEM(queries.shape, BF16),
         pltpu.VMEM((2, 4, 4, 576, 128), BF16),
         pltpu.VMEM((2, 4, 4, 576, 128), BF16),
         pltpu.VMEM((2, 2, 2, 576, 128), BF16),
@@ -588,7 +597,7 @@
     scratch += rings(4, (4,), 896)
     scratch += rings(4, (4,), 1792)
     scratch.append(pltpu.VMEM((4, 3, 8, 1792), BF16))
-    scratch += [dma((48,)), dma((48,)), dma((30,)), dma((30,)), dma((32,)), dma((32,)), dma((9,))]
+    scratch += [dma((48,)), dma((48,)), dma((30,)), dma((30,)), dma((32,)), dma((32,)), dma((11,))]
     stream, normed, mix = pl.pallas_call(
         attention_kernel,
         out_shape=(
@@ -596,7 +605,7 @@
             jax.ShapeDtypeStruct((8, model), BF16),
             jax.ShapeDtypeStruct((8, 128), BF16),
         ),
-        in_specs=[smem, smem, smem, vmem, vmem, vmem, vmem, hbm, vmem, vmem, vmem, vmem],
+        in_specs=[smem, smem, smem, hbm, hbm, vmem, vmem, hbm, vmem, vmem, vmem, vmem],
         out_specs=(vmem, vmem, vmem),
         scratch_shapes=scratch,
         compiler_params=pltpu.CompilerParams(

time: 172 us -> 172 us (level)
  no operation moved by 1% of the time
where the time goes in v7:
time: 172 us; the launch traced here: 171 us
  Pallas kernels  170 us (99%)
    pallas_call x1, Pallas kernels, per_device(): pl.pallas_call(attention_kernel, out_shape=(jax.ShapeDtypeStruct((8, mode...  92.1 us
    pallas_call x1, Pallas kernels, per_device(): pl.pallas_call(expert_kernel, out_shape=jax.ShapeDtypeStruct(residual.sha...  77.7 us

profile of v7, /device:TPU:0, one launch (start us, length us, event | category | flops | bytes accessed | tf_op | source)
XLA Modules:
  0.0 171.4 jit_solution(14993744221347741622)
XLA Ops:
  0.0 92.1 %attention.1 = (bf16[8,7168]{1,0:T(8,128)(2,1)}, bf16[8,7168]{1,0:T(8,128)(2,1)}, bf16[8,128]{1,0:T(8,128)(2,1)}) custom-call(s32[1,2,16]{2,1,0:T(2,128)} %bitcast.3, s32[4,8]{1,0:T(4,128)} %tab.1, s32[4]{0:T(128)} %lens.1, bf16[24,576,128]{2,1,0:T(8,128)(2,1)} %pool_hbm.1, bf16[2,4,64,576]{3,2,1,0:T(8,128)(2,1)} %queries_hbm.1, ...), custom_call_target="tpu_custom_call" | custom-call | tf_op jit(solution)/shard_map/attention/pallas_call | solution.py:601
  92.1 77.7 %experts.1 = bf16[2,4,7168]{2,1,0:T(4,128)(2,1)} custom-call(bf16[8,7168]{1,0:T(8,128)(2,1)} %get-tuple-element.8.normed, bf16[8,128]{1,0:T(8,128)(2,1)} %get-tuple-element.9.mix, bf16[8,7168]{1,0:T(8,128)(2,1)} %get-tuple-element.10.stream, bf16[2,7168,128]{2,1,0:T(8,128)(2,1)} %gate.1, bf16[2,7168,128]{2,1,0:T(8,128)(2,1)} %up.1, bf16[2,128,7168]{2,1,0:T(8,128)(2,1)} %down.1), custom_call_target="tpu_custom_call" | custom-call | tf_op jit(solution)/shard_map/experts/pallas_call | solution.py:632
  169.8 1.6 copy.17
